TPU v7x, 512 devices: a whole 4x8x8 slice. The times are simulated.
512 devices in a mesh: bead: 16 (over x_lo, z), dom: 32 (over x_hi, y, core).
Axes of the slice: x: 4 (x_hi: 2, x_lo: 2; x = x_hi * 2 + x_lo), y: 8, z: 8, core: 2. Of those that a mesh axis runs over, the one named last changes fastest.
Arguments:
- positions: float32 [32, 24, 128, 128], P('bead', None, 'dom'), may hold values from -6 to 6
- momenta: float32 [32, 24, 128, 128], P('bead', None, 'dom'), may hold values from -6 to 6
- offsets: int32 [27], replicated, may hold values from 0 to 26, each once
- harmonic: float32 [24, 648], replicated, may hold values from -0.25 to 0.25
- cubic: float32 [576, 648], replicated, may hold values from -0.046875 to 0.046875
Outputs:
- new_positions: float32 [32, 24, 128, 128], P('bead', None, 'dom')
- new_momenta: float32 [32, 24, 128, 128], P('bead', None, 'dom')
Inputs may be any that keep to these rules, and one draw needn't show every extreme that they name: A permutation of the 27 offsets: each cell offset with components in -1, 0, 1 is named once.
All inputs are finite; a program needn't handle non-finite values.
Results may differ from a plain program's by a relative error of at most 0.00007.
Values sent between devices are 32-bit elements; how exact they have to be, the bound alone decides.
No kernel may reach another device: no remote copies, remote signals or barrier semaphores. Data moves between devices by JAX's collectives and lax.ppermute only.
A program may use at most 128 MiB of HBM per device.

v0:
```python
import functools

import jax
import jax.numpy as jnp
import numpy as np
from jax import lax
from jax.experimental import pallas as pl
from jax.experimental.pallas import tpu as pltpu
from jax.sharding import PartitionSpec as P

BEADS = 32
COMP = 24
NOFF = 27
CZ = 16
CELLS = 128
OWN = 4
EXT = OWN + 2
BLOCK = 224
PLANE = 3 * BLOCK
DEPTH = 2048
ROWS = 608
TIME_STEP = 0.5
CYCLE_FREQ = 1.0
KICK = 0.5 * TIME_STEP

VMEM = pl.BlockSpec(memory_space=pltpu.VMEM)
SMEM = pl.BlockSpec(memory_space=pltpu.SMEM)
f32 = jnp.float32
bf16 = jnp.bfloat16


def propagator(groups):
    count = BEADS
    rows = np.arange(count)[:, None] * 1.0
    cols = np.arange(count)[None, :]
    angle = 2.0 * np.pi * rows * cols / count
    table = np.where(
        cols == 0,
        1.0 / np.sqrt(count) + 0.0 * angle,
        np.where(
            cols < count // 2,
            np.sqrt(2.0 / count) * np.cos(angle),
            np.where(
                cols == count // 2,
                np.cos(np.pi * rows) / np.sqrt(count),
                np.sqrt(2.0 / count) * np.sin(angle),
            ),
        ),
    )
    freq = 2.0 * CYCLE_FREQ * np.sin(np.pi * np.arange(count) / count)
    cosine = np.cos(freq * TIME_STEP)
    sine_over = np.where(
        freq > 0, np.sin(freq * TIME_STEP) / np.where(freq > 0, freq, 1.0), TIME_STEP
    )
    spring = freq * np.sin(freq * TIME_STEP)
    turn = (table * cosine) @ table.T
    drift = (table * sine_over) @ table.T
    pull = (table * spring) @ table.T
    whole = np.block([[turn, drift], [-pull, turn]])
    per = count // groups
    order = np.arange(2 * count).reshape(2, groups, per).transpose(0, 2, 1).reshape(-1)
    return whole[np.ix_(order, order)].astype(np.float32)


def put_neighbours(ns_ref, slot, bead, field):
    z = lax.broadcasted_iota(jnp.int32, field.shape, 1) % CZ
    up = jnp.where(z == CZ - 1, pltpu.roll(field, CZ - 1, 1), pltpu.roll(field, CELLS - 1, 1))
    down = jnp.where(z == 0, pltpu.roll(field, CELLS - CZ + 1, 1), pltpu.roll(field, 1, 1))
    along_z = [down, field, up]
    parts = [pltpu.roll(v, CZ, 1) for v in along_z]
    parts += along_z
    parts += [pltpu.roll(v, CELLS - CZ, 1) for v in along_z]
    parts.append(jnp.zeros((BLOCK - 9 * COMP, CELLS), f32))
    stack = jnp.concatenate(parts, 0)
    high = stack.astype(bf16)
    low = (stack - high.astype(f32)).astype(bf16)
    lanes = pl.ds(bead * CELLS, CELLS)
    ns_ref[pl.ds(slot * PLANE, BLOCK), lanes] = high
    ns_ref[pl.ds(slot * PLANE + BLOCK, BLOCK), lanes] = low
    ns_ref[pl.ds(slot * PLANE + 2 * BLOCK, BLOCK), lanes] = high


def force_of(w_ref, ns_ref, slot, own):
    rows = jnp.dot(w_ref[...], ns_ref[pl.ds(slot * PLANE, DEPTH), :], preferred_element_type=f32)
    higher = rows[: COMP * COMP].reshape(COMP, COMP, 2 * CELLS)
    anharm = jnp.sum(higher * own[None, :, :], axis=1)
    return -(rows[COMP * COMP : COMP * COMP + COMP] + anharm)


def own_plane(ref, bead, plane):
    return ref[pl.ds(bead * COMP * OWN + plane, COMP, stride=OWN), :]


def pack_kernel(pos_ref, mom_ref, left_ref, right_ref):
    for bead in range(2):
        for place, ref, first, last in (
            (0, pos_ref, 0, 2),
            (1, pos_ref, 1, 3),
            (2, mom_ref, 0, 3),
        ):
            rows = pl.ds((place * 2 + bead) * COMP, COMP)
            left_ref[rows, :] = own_plane(ref, bead, first)
            right_ref[rows, :] = own_plane(ref, bead, last)


def inner_kernel(off_ref, harm_ref, cub_ref, pos_ref, mom_ref, w_ref, half_ref, hpad, hturn, wt, cat, ns):
    hpad[...] = jnp.zeros_like(hpad)
    hpad[64 : 64 + COMP, 0 : NOFF * COMP] = harm_ref[...]
    for tile in range(6):
        hturn[tile * 128 : (tile + 1) * 128, :] = hpad[:, tile * 128 : (tile + 1) * 128].T
    for dx in range(3):
        wt[dx * BLOCK + 9 * COMP : (dx + 1) * BLOCK, :] = jnp.zeros((8, 640), f32)
    for o in range(NOFF):
        code = off_ref[o]
        rows = pl.ds(pl.multiple_of(code * COMP + (code // 9) * 8, 8), COMP)
        wt[rows, 512:640] = hturn[o * COMP : (o + 1) * COMP, :]
        wt[rows, 0 : COMP * COMP] = cub_ref[o * COMP : (o + 1) * COMP, :]
    for dx in range(3):
        block = wt[dx * BLOCK : (dx + 1) * BLOCK, :]
        high = block.astype(bf16)
        low = (block - high.astype(f32)).astype(bf16)
        cat[dx * PLANE : dx * PLANE + BLOCK, :] = high
        cat[dx * PLANE + BLOCK : dx * PLANE + 2 * BLOCK, :] = high
        cat[dx * PLANE + 2 * BLOCK : (dx + 1) * PLANE, :] = low
    cat[3 * PLANE : DEPTH, :] = jnp.zeros((DEPTH - 3 * PLANE, 640), bf16)
    for m in range(5):
        size = min(128, ROWS - m * 128)
        for k in range(DEPTH // 128):
            turned = cat[k * 128 : (k + 1) * 128, m * 128 : (m + 1) * 128].T
            w_ref[m * 128 : m * 128 + size, k * 128 : (k + 1) * 128] = turned[:size]
    ns[OWN * PLANE : OWN * PLANE + 32, :] = jnp.zeros((32, 2 * CELLS), bf16)
    for plane in range(OWN):
        for bead in range(2):
            put_neighbours(ns, plane, bead, own_plane(pos_ref, bead, plane))
    for plane in (1, 2):
        own = jnp.concatenate([own_plane(pos_ref, bead, plane) for bead in range(2)], 1)
        mom = jnp.concatenate([own_plane(mom_ref, bead, plane) for bead in range(2)], 1)
        half_ref[(plane - 1) * COMP : plane * COMP, :] = mom + KICK * force_of(w_ref, ns, plane - 1, own)


def outer_kernel(w_ref, pos_ref, mom_ref, half_ref, left_ref, right_ref, send_ref, ns):
    def block(ref, place, bead):
        return ref[(place * 2 + bead) * COMP : (place * 2 + bead + 1) * COMP, :]

    def position(plane, bead):
        if plane < 0:
            return block(left_ref, plane + 2, bead)
        if plane >= OWN:
            return block(right_ref, plane - OWN, bead)
        return own_plane(pos_ref, bead, plane)

    def momentum(plane, bead):
        if plane < 0:
            return block(left_ref, 2, bead)
        if plane >= OWN:
            return block(right_ref, 2, bead)
        return own_plane(mom_ref, bead, plane)

    def store(plane, kind, bead, value):
        send_ref[pl.ds((plane + 1) * COMP * 4 + kind * 2 + bead, COMP, stride=4), :] = value

    ns[8 * PLANE : 8 * PLANE + 32, :] = jnp.zeros((32, 2 * CELLS), bf16)
    for plane in range(-2, OWN + 2):
        for bead in range(2):
            put_neighbours(ns, plane + 2, bead, position(plane, bead))
    for plane in range(-1, OWN + 1):
        for bead in range(2):
            store(plane, 0, bead, position(plane, bead))
    for plane in (1, 2):
        for bead in range(2):
            store(plane, 1, bead, half_ref[(plane - 1) * COMP : plane * COMP, bead * CELLS : (bead + 1) * CELLS])
    for plane in (-1, 0, OWN - 1, OWN):
        own = jnp.concatenate([position(plane, bead) for bead in range(2)], 1)
        force = force_of(w_ref, ns, plane + 1, own)
        for bead in range(2):
            half = momentum(plane, bead) + KICK * force[:, bead * CELLS : (bead + 1) * CELLS]
            store(plane, 1, bead, half)


def bead_kernel(groups, rows, map_ref, in_ref, out_ref):
    columns = []
    for r in range(rows):
        columns.append(
            jnp.concatenate([in_ref[pl.ds(r * 4 + q, groups, stride=rows * 4), :] for q in range(4)], 0)
        )
    moved = jnp.dot(
        map_ref[...],
        jnp.concatenate(columns, 1),
        precision=lax.Precision.HIGHEST,
        preferred_element_type=f32,
    )
    for r in range(rows):
        for q in range(4):
            out_ref[pl.ds(r * 4 + q, groups, stride=rows * 4), :] = moved[
                q * groups : (q + 1) * groups, r * CELLS : (r + 1) * CELLS
            ]


def last_kernel(w_ref, in_ref, pos_ref, mom_ref, ns):
    def value(plane, kind, bead):
        return in_ref[pl.ds(plane * COMP * 4 + kind * 2 + bead, COMP, stride=4), :]

    ns[EXT * PLANE : EXT * PLANE + 32, :] = jnp.zeros((32, 2 * CELLS), bf16)
    for plane in range(EXT):
        for bead in range(2):
            field = value(plane, 0, bead)
            put_neighbours(ns, plane, bead, field)
            if 1 <= plane <= OWN:
                pos_ref[pl.ds(bead * COMP * OWN + plane - 1, COMP, stride=OWN), :] = field
    for plane in range(1, OWN + 1):
        own = jnp.concatenate([value(plane, 0, bead) for bead in range(2)], 1)
        force = force_of(w_ref, ns, plane - 1, own)
        for bead in range(2):
            mom_ref[pl.ds(bead * COMP * OWN + plane - 1, COMP, stride=OWN), :] = (
                value(plane, 1, bead) + KICK * force[:, bead * CELLS : (bead + 1) * CELLS]
            )


def call(kernel, name, ins, outs, scratch, flops, *args):
    size = sum(int(np.prod(a.shape)) * a.dtype.itemsize for a in (*args, *outs))
    return pl.pallas_call(
        kernel,
        name=name,
        in_specs=ins,
        out_specs=[VMEM] * len(outs),
        out_shape=list(outs),
        scratch_shapes=scratch,
        compiler_params=pltpu.CompilerParams(vmem_limit_bytes=24 * 1024 * 1024),
        cost_estimate=pl.CostEstimate(flops=flops, bytes_accessed=size, transcendentals=0),
    )(*args)


def neighbours(planes):
    return pltpu.VMEM((planes * PLANE + 32, 2 * CELLS), bf16)


def body(positions, momenta, offsets, harmonic, cubic):
    shape = jax.ShapeDtypeStruct
    per_plane = 2 * ROWS * DEPTH * 2 * CELLS
    groups = lax.axis_size("bead")
    doms = lax.axis_size("dom")
    pos = positions.reshape(2 * COMP * OWN, CELLS)
    mom = momenta.reshape(2 * COMP * OWN, CELLS)
    planes = shape((6 * COMP, CELLS), f32)
    to_left, to_right = call(pack_kernel, "pack", [VMEM] * 2, [planes] * 2, [], 0, pos, mom)
    from_left = lax.ppermute(to_right, "dom", [(i, (i + 1) % doms) for i in range(doms)])
    from_right = lax.ppermute(to_left, "dom", [((i + 1) % doms, i) for i in range(doms)])
    weights, half = call(
        inner_kernel,
        "inner",
        [SMEM] + [VMEM] * 4,
        [shape((ROWS, DEPTH), bf16), shape((2 * COMP, 2 * CELLS), f32)],
        [
            pltpu.VMEM((128, 768), f32),
            pltpu.VMEM((768, 128), f32),
            pltpu.VMEM((PLANE, 640), f32),
            pltpu.VMEM((DEPTH, 640), bf16),
            neighbours(OWN),
        ],
        2 * per_plane,
        offsets,
        harmonic,
        cubic.T,
        pos,
        mom,
    )
    rows = EXT * COMP // groups
    exchanged = shape((groups * rows * 4, CELLS), f32)
    (send,) = call(
        outer_kernel, "outer", [VMEM] * 6, [exchanged], [neighbours(8)], 4 * per_plane,
        weights, pos, mom, half, from_left, from_right,
    )

    def swap(x):
        x = lax.all_to_all(x.reshape(groups, rows, 4, CELLS), "bead", 0, 0, tiled=True)
        return x.reshape(groups * rows * 4, CELLS)

    (back,) = call(
        functools.partial(bead_kernel, groups, rows), "beads", [VMEM] * 2, [exchanged], [],
        2 * 64 * 64 * 6 * rows * CELLS, jnp.asarray(propagator(groups)), swap(send),
    )
    own = shape((2 * COMP * OWN, CELLS), f32)
    new_pos, new_mom = call(
        last_kernel, "last", [VMEM] * 2, [own] * 2, [neighbours(EXT)], 4 * per_plane, weights, swap(back)
    )
    return new_pos.reshape(positions.shape), new_mom.reshape(momenta.shape)


def solution(mesh):
    return jax.shard_map(
        body,
        mesh=mesh,
        in_specs=(P("bead", None, "dom", None), P("bead", None, "dom", None), P(), P(), P()),
        out_specs=(P("bead", None, "dom", None), P("bead", None, "dom", None)),
        check_vma=False,
    )
```

profile of v0, /device:TPU:24, one launch (start us, length us, event | category | flops | bytes accessed | tf_op | source)
XLA Modules:
  0.0 61.4 jit_solution(13906023538624479918)
XLA Ops:
  0.6 0.0 copy-start
  0.6 0.9 %copy-done = f32[2,24,4,128]{3,2,1,0:T(4,128)S(1)} copy-done((f32[2,24,4,128]{3,2,1,0:T(4,128)S(1)}, f32[2,24,4,128]{3,2,1,0:T(4,128)}, u32[]{:S(2)}) %copy-start) | copy-done | bytes 98328
  1.5 0.0 copy-start.3
  1.5 0.9 %copy-done.3 = f32[2,24,4,128]{3,2,1,0:T(4,128)S(1)} copy-done((f32[2,24,4,128]{3,2,1,0:T(4,128)S(1)}, f32[2,24,4,128]{3,2,1,0:T(4,128)}, u32[]{:S(2)}) %copy-start.3) | copy-done | bytes 98328
  2.4 0.0 copy-start.2
  2.4 0.0 copy-start.5
  2.4 2.1 %collective-permute-start = (f32[144,128]{1,0:T(8,128)S(1)}, f32[144,128]{1,0:T(8,128)S(1)}, u32[]{:S(2)}, u32[]{:S(2)}) collective-permute-start(f32[144,128]{1,0:T(8,128)S(1)} %get-tuple-element.10), channel_id=1, source_target_pairs={{0,1},{1,2},{2,3},{3,4},{4,5},{5,6},{6,7},{7,8},{8,9},{9,10},{10,1... | collective-permute-start | bytes 221192 | tf_op jit(solution)/shard_map/ppermute | solution.py:246
  4.5 3.6 %collective-permute-start.1 = (f32[144,128]{1,0:T(8,128)S(1)}, f32[144,128]{1,0:T(8,128)S(1)}, u32[]{:S(2)}, u32[]{:S(2)}) collective-permute-start(f32[144,128]{1,0:T(8,128)S(1)} %get-tuple-element.11), channel_id=1, source_target_pairs={{1,0},{2,1},{3,2},{4,3},{5,4},{6,5},{7,6},{8,7},{9,8},{10,9},{11,1... | collective-permute-start | bytes 221192 | tf_op jit(solution)/shard_map/ppermute | solution.py:247
  8.1 0.0 copy-start.1
  8.2 0.9 %copy-done.1 = f32[2,24,4,128]{3,2,1,0:T(4,128)S(1)} copy-done((f32[2,24,4,128]{3,2,1,0:T(4,128)S(1)}, f32[2,24,4,128]{3,2,1,0:T(4,128)}, u32[]{:S(2)}) %copy-start.1) | copy-done | bytes 98328
  9.0 0.0 copy-start.4
  9.0 0.9 %copy-done.4 = f32[2,24,4,128]{3,2,1,0:T(4,128)S(1)} copy-done((f32[2,24,4,128]{3,2,1,0:T(4,128)S(1)}, f32[2,24,4,128]{3,2,1,0:T(4,128)}, u32[]{:S(2)}) %copy-start.4) | copy-done | bytes 98328
  9.9 0.0 copy-start.7
  9.9 1.4 %copy-done.7 = f32[576,648]{0,1:T(8,128)S(1)} copy-done((f32[576,648]{0,1:T(8,128)S(1)}, f32[576,648]{0,1:T(8,128)}, u32[]{:S(2)}) %copy-start.7) | copy-done | bytes 1493016
  11.4 0.0 copy-start.8
  11.4 0.9 %copy-done.8 = f32[24,648]{1,0:T(8,128)S(1)} copy-done((f32[24,648]{1,0:T(8,128)S(1)}, f32[24,648]{1,0:T(8,128)}, u32[]{:S(2)}) %copy-start.8) | copy-done | bytes 62232
  12.3 0.0 copy-start.9
  12.3 0.7 %copy-done.9 = s32[27]{0:T(128)S(1)} copy-done((s32[27]{0:T(128)S(1)}, s32[27]{0:T(128)}, u32[]{:S(2)}) %copy-start.9) | copy-done | bytes 132
  12.9 2.6 %inner.1 = (bf16[608,2048]{1,0:T(8,128)(2,1)S(1)}, f32[48,256]{1,0:T(8,128)S(1)}) custom-call(s32[27]{0:T(128)S(1)} %copy-done.9, f32[24,648]{1,0:T(8,128)S(1)} %copy-done.8, f32[648,576]{1,0:T(8,128)S(1)} %bitcast.19, f32[192,128]{1,0:T(8,128)S(1)} %bitcast.14, f32[192,128]{1,0:T(8,128)S(1)} %bitcast.17), custom_call_target="tpu_custom_call" | custom-call | flops 1275068416 | bytes 4291436 | tf_op jit(solution)/shard_map/inner/pallas_call | solution.py:221
  15.5 0.0 collective-permute-done.left_ref
  15.5 0.0 collective-permute-done.1.right_ref
  15.5 0.0 copy-done.2
  15.6 0.0 copy-done.5
  15.6 0.0 copy-start.6
  15.6 3.1 %outer.1 = f32[576,128]{1,0:T(8,128)S(1)} custom-call(bf16[608,2048]{1,0:T(8,128)(2,1)S(1)} %get-tuple-element.8.w_ref, f32[192,128]{1,0:T(8,128)S(1)} %bitcast.15, f32[192,128]{1,0:T(8,128)S(1)} %bitcast.18, f32[48,256]{1,0:T(8,128)S(1)} %get-tuple-element.9.half_ref, f32[144,128]{1,0:T(8,128)S(1)} %collective-permute-done.left_ref, ...), custom_call_target="tpu_custom_call" | custom-call | flops 2550136832 | bytes 3178496 | tf_op jit(solution)/shard_map/outer/pallas_call | solution.py:221
  18.7 23.1 %all_to_all.10 = f32[16,9,4,128]{3,2,1,0:T(4,128)S(1)} all-to-all(f32[16,9,4,128]{3,2,1,0:T(4,128)S(1)} %bitcast.12), channel_id=1, replica_groups=mesh['bead'=16,'dom'=32] {'bead'}, dimensions={0} | all-to-all | bytes 589824 | tf_op jit(solution)/shard_map/all_to_all | solution.py:275
  41.7 0.0 copy-done.6
  41.7 0.4 beads.1
  42.1 15.6 %all_to_all.11 = f32[16,9,4,128]{3,2,1,0:T(4,128)S(1)} all-to-all(f32[16,9,4,128]{3,2,1,0:T(4,128)S(1)} %bitcast.10), channel_id=1, replica_groups=mesh['bead'=16,'dom'=32] {'bead'}, dimensions={0} | all-to-all | bytes 589824 | tf_op jit(solution)/shard_map/all_to_all | solution.py:275
  57.7 3.7 %last.1 = (f32[192,128]{1,0:T(8,128)}, f32[192,128]{1,0:T(8,128)}) custom-call(bf16[608,2048]{1,0:T(8,128)(2,1)S(1)} %get-tuple-element.8.w_ref, f32[576,128]{1,0:T(8,128)S(1)} %bitcast.11), custom_call_target="tpu_custom_call" | custom-call | flops 2550136832 | bytes 2981888 | tf_op jit(solution)/shard_map/last/pallas_call | solution.py:221
  (1 shorter events, 0.0 us)
Async XLA Ops:
  0.6 0.9 %copy-start = (f32[2,24,4,128]{3,2,1,0:T(4,128)S(1)}, f32[2,24,4,128]{3,2,1,0:T(4,128)}, u32[]{:S(2)}) copy-start(f32[2,24,4,128]{3,2,1,0:T(4,128)} %param.6) | copy-start | bytes 294916
  1.5 0.9 %copy-start.3 = (f32[2,24,4,128]{3,2,1,0:T(4,128)S(1)}, f32[2,24,4,128]{3,2,1,0:T(4,128)}, u32[]{:S(2)}) copy-start(f32[2,24,4,128]{3,2,1,0:T(4,128)} %param.7) | copy-start | bytes 294916
  2.4 13.1 %copy-start.2 = (f32[2,24,4,128]{3,2,1,0:T(4,128)S(1)}, f32[2,24,4,128]{3,2,1,0:T(4,128)}, u32[]{:S(2)}) copy-start(f32[2,24,4,128]{3,2,1,0:T(4,128)} %param.6) | copy-start | bytes 294916
  2.4 13.1 %copy-start.5 = (f32[2,24,4,128]{3,2,1,0:T(4,128)S(1)}, f32[2,24,4,128]{3,2,1,0:T(4,128)}, u32[]{:S(2)}) copy-start(f32[2,24,4,128]{3,2,1,0:T(4,128)} %param.7) | copy-start | bytes 294916
  2.4 13.1 %collective-permute-start = (f32[144,128]{1,0:T(8,128)S(1)}, f32[144,128]{1,0:T(8,128)S(1)}, u32[]{:S(2)}, u32[]{:S(2)}) collective-permute-start(f32[144,128]{1,0:T(8,128)S(1)} %get-tuple-element.10), channel_id=1, source_target_pairs={{0,1},{1,2},{2,3},{3,4},{4,5},{5,6},{6,7},{7,8},{8,9},{9,10},{10,1... | collective-permute-start | bytes 221192 | tf_op jit(solution)/shard_map/ppermute | solution.py:246
  4.5 11.0 %collective-permute-start.1 = (f32[144,128]{1,0:T(8,128)S(1)}, f32[144,128]{1,0:T(8,128)S(1)}, u32[]{:S(2)}, u32[]{:S(2)}) collective-permute-start(f32[144,128]{1,0:T(8,128)S(1)} %get-tuple-element.11), channel_id=1, source_target_pairs={{1,0},{2,1},{3,2},{4,3},{5,4},{6,5},{7,6},{8,7},{9,8},{10,9},{11,1... | collective-permute-start | bytes 221192 | tf_op jit(solution)/shard_map/ppermute | solution.py:247
  8.1 0.9 %copy-start.1 = (f32[2,24,4,128]{3,2,1,0:T(4,128)S(1)}, f32[2,24,4,128]{3,2,1,0:T(4,128)}, u32[]{:S(2)}) copy-start(f32[2,24,4,128]{3,2,1,0:T(4,128)} %param.6) | copy-start | bytes 294916
  9.0 0.9 %copy-start.4 = (f32[2,24,4,128]{3,2,1,0:T(4,128)S(1)}, f32[2,24,4,128]{3,2,1,0:T(4,128)}, u32[]{:S(2)}) copy-start(f32[2,24,4,128]{3,2,1,0:T(4,128)} %param.7) | copy-start | bytes 294916
  9.9 1.4 %copy-start.7 = (f32[576,648]{0,1:T(8,128)S(1)}, f32[576,648]{0,1:T(8,128)}, u32[]{:S(2)}) copy-start(f32[576,648]{0,1:T(8,128)} %param.10) | copy-start | bytes 4478980
  11.4 0.9 %copy-start.8 = (f32[24,648]{1,0:T(8,128)S(1)}, f32[24,648]{1,0:T(8,128)}, u32[]{:S(2)}) copy-start(f32[24,648]{1,0:T(8,128)} %harm_ref.1) | copy-start | bytes 186628
  12.3 0.7 %copy-start.9 = (s32[27]{0:T(128)S(1)}, s32[27]{0:T(128)}, u32[]{:S(2)}) copy-start(s32[27]{0:T(128)} %off_ref.1) | copy-start | bytes 328
  15.6 26.2 %copy-start.6 = (f32[64,64]{1,0:T(8,128)S(1)}, f32[64,64]{1,0:T(8,128)}, u32[]{:S(2)}) copy-start(f32[64,64]{1,0:T(8,128)} %constant.2.clone.map_ref) | copy-start | bytes 49156
where the time goes:
time: 61.8 us; the launch traced here: 61.4 us
  blocking collectives  38.7 us (63%)
  Pallas kernels  9.72 us (16%)
  local copies, waits for them, and re-layouts  6.55 us (11%)
  starting transfers between devices  5.69 us (9%)
  between operations  0.73 us (1%)
    all_to_all x2, blocking collectives, swap(): lax.all_to_all(x.reshape(groups, rows, 4, CELLS), 'bead', 0, 0, tiled=True)  38.7 us
    pallas_call x5, Pallas kernels, call(): pl.pallas_call(kernel, name=name, in_specs=ins, out_specs=[VMEM] * len(ou...  9.72 us
    unnamed x20, local copies, waits for them, and re-layouts  6.55 us
    ppermute x1, starting transfers between devices, body(): lax.ppermute(to_left, 'dom', [((i + 1) % doms, i) for i in range(doms)])  3.64 us
    ppermute x1, starting transfers between devices, body(): lax.ppermute(to_right, 'dom', [(i, (i + 1) % doms) for i in range(doms)])  2.05 us
  transfers between devices with their start and end apart: 2, of which 0 were waited for; matrix products, arithmetic and copies ran while one was open for 0% of the time, Pallas kernels for 4%

commit v1 on v0

--- a/solution.py
+++ b/solution.py
@@ -1,5 +1,3 @@
-import functools
-
 import jax
 import jax.numpy as jnp
 import numpy as np
@@ -23,8 +21,10 @@
 CYCLE_FREQ = 1.0
 KICK = 0.5 * TIME_STEP
 
+EARLY = 10_000_000_000
+GROUP = 16
+SMEM = pl.BlockSpec(memory_space=pltpu.SMEM)
 VMEM = pl.BlockSpec(memory_space=pltpu.VMEM)
-SMEM = pl.BlockSpec(memory_space=pltpu.SMEM)
 f32 = jnp.float32
 bf16 = jnp.bfloat16
 
@@ -87,23 +87,41 @@
     return -(rows[COMP * COMP : COMP * COMP + COMP] + anharm)
 
 
+def halves(core, here, there):
+    return jnp.where(core == 0, here, there)
+
+
 def own_plane(ref, bead, plane):
     return ref[pl.ds(bead * COMP * OWN + plane, COMP, stride=OWN), :]
 
 
-def pack_kernel(pos_ref, mom_ref, left_ref, right_ref):
+def block(ref, place, bead):
+    return ref[(place * 2 + bead) * COMP : (place * 2 + bead + 1) * COMP, :]
+
+
+def planes_kernel(ref, planes_ref):
+    for plane in range(OWN):
+        for bead in range(2):
+            planes_ref[pl.ds((plane * 2 + bead) * COMP, COMP), :] = own_plane(ref, bead, plane)
+
+
+def pack_kernel(pos_ref, raw_ref, far_ref, near_ref, mom_ref):
+    core = lax.axis_index("dom") % 2
+    planes_kernel(raw_ref, mom_ref)
     for bead in range(2):
-        for place, ref, first, last in (
-            (0, pos_ref, 0, 2),
-            (1, pos_ref, 1, 3),
-            (2, mom_ref, 0, 3),
-        ):
+        pos = [block(pos_ref, plane, bead) for plane in range(OWN)]
+        first, last = block(mom_ref, 0, bead), block(mom_ref, OWN - 1, bead)
+        for place, left, right in ((0, pos[0], pos[2]), (1, pos[1], pos[3]), (2, first, last)):
             rows = pl.ds((place * 2 + bead) * COMP, COMP)
-            left_ref[rows, :] = own_plane(ref, bead, first)
-            right_ref[rows, :] = own_plane(ref, bead, last)
+            far_ref[rows, :] = halves(core, left, right)
+            near_ref[rows, :] = halves(core, right, left)
 
 
 def inner_kernel(off_ref, harm_ref, cub_ref, pos_ref, mom_ref, w_ref, half_ref, hpad, hturn, wt, cat, ns):
+    ns[OWN * PLANE : OWN * PLANE + 32, :] = jnp.zeros((32, 2 * CELLS), bf16)
+    for plane in range(OWN):
+        for bead in range(2):
+            put_neighbours(ns, plane, bead, block(pos_ref, plane, bead))
     hpad[...] = jnp.zeros_like(hpad)
     hpad[64 : 64 + COMP, 0 : NOFF * COMP] = harm_ref[...]
     for tile in range(6):
@@ -116,9 +134,9 @@
         wt[rows, 512:640] = hturn[o * COMP : (o + 1) * COMP, :]
         wt[rows, 0 : COMP * COMP] = cub_ref[o * COMP : (o + 1) * COMP, :]
     for dx in range(3):
-        block = wt[dx * BLOCK : (dx + 1) * BLOCK, :]
-        high = block.astype(bf16)
-        low = (block - high.astype(f32)).astype(bf16)
+        rows = wt[dx * BLOCK : (dx + 1) * BLOCK, :]
+        high = rows.astype(bf16)
+        low = (rows - high.astype(f32)).astype(bf16)
         cat[dx * PLANE : dx * PLANE + BLOCK, :] = high
         cat[dx * PLANE + BLOCK : dx * PLANE + 2 * BLOCK, :] = high
         cat[dx * PLANE + 2 * BLOCK : (dx + 1) * PLANE, :] = low
@@ -128,36 +146,38 @@
         for k in range(DEPTH // 128):
             turned = cat[k * 128 : (k + 1) * 128, m * 128 : (m + 1) * 128].T
             w_ref[m * 128 : m * 128 + size, k * 128 : (k + 1) * 128] = turned[:size]
-    ns[OWN * PLANE : OWN * PLANE + 32, :] = jnp.zeros((32, 2 * CELLS), bf16)
-    for plane in range(OWN):
-        for bead in range(2):
-            put_neighbours(ns, plane, bead, own_plane(pos_ref, bead, plane))
     for plane in (1, 2):
-        own = jnp.concatenate([own_plane(pos_ref, bead, plane) for bead in range(2)], 1)
-        mom = jnp.concatenate([own_plane(mom_ref, bead, plane) for bead in range(2)], 1)
+        own = jnp.concatenate([block(pos_ref, plane, bead) for bead in range(2)], 1)
+        mom = jnp.concatenate([block(mom_ref, plane, bead) for bead in range(2)], 1)
         half_ref[(plane - 1) * COMP : plane * COMP, :] = mom + KICK * force_of(w_ref, ns, plane - 1, own)
 
 
-def outer_kernel(w_ref, pos_ref, mom_ref, half_ref, left_ref, right_ref, send_ref, ns):
-    def block(ref, place, bead):
-        return ref[(place * 2 + bead) * COMP : (place * 2 + bead + 1) * COMP, :]
+def place_of(plane):
+    return (0, plane) if plane < 3 else (1, EXT - 1 - plane)
+
+
+def outer_kernel(w_ref, pos_ref, mom_ref, half_ref, far_ref, near_ref, send_ref, ns):
+    core = lax.axis_index("dom") % 2
+    left = [[halves(core, block(far_ref, i, bead), block(near_ref, i, bead)) for bead in range(2)] for i in range(3)]
+    right = [[halves(core, block(near_ref, i, bead), block(far_ref, i, bead)) for bead in range(2)] for i in range(3)]
 
     def position(plane, bead):
         if plane < 0:
-            return block(left_ref, plane + 2, bead)
+            return left[plane + 2][bead]
         if plane >= OWN:
-            return block(right_ref, plane - OWN, bead)
-        return own_plane(pos_ref, bead, plane)
+            return right[plane - OWN][bead]
+        return block(pos_ref, plane, bead)
 
     def momentum(plane, bead):
         if plane < 0:
-            return block(left_ref, 2, bead)
+            return left[2][bead]
         if plane >= OWN:
-            return block(right_ref, 2, bead)
-        return own_plane(mom_ref, bead, plane)
+            return right[2][bead]
+        return block(mom_ref, plane, bead)
 
     def store(plane, kind, bead, value):
-        send_ref[pl.ds((plane + 1) * COMP * 4 + kind * 2 + bead, COMP, stride=4), :] = value
+        half, step = place_of(plane + 1)
+        send_ref[pl.ds(half * 288 + step * 4 + kind * 2 + bead, COMP, stride=12), :] = value
 
     ns[8 * PLANE : 8 * PLANE + 32, :] = jnp.zeros((32, 2 * CELLS), bf16)
     for plane in range(-2, OWN + 2):
@@ -177,28 +197,31 @@
             store(plane, 1, bead, half)
 
 
-def bead_kernel(groups, rows, map_ref, in_ref, out_ref):
+def bead_kernel(map_ref, in_ref, out_ref):
     columns = []
-    for r in range(rows):
-        columns.append(
-            jnp.concatenate([in_ref[pl.ds(r * 4 + q, groups, stride=rows * 4), :] for q in range(4)], 0)
-        )
+    for r in range(9):
+        columns.append(jnp.concatenate([in_ref[pl.ds(r * 4 + q, GROUP, stride=36), :] for q in range(4)], 0))
     moved = jnp.dot(
         map_ref[...],
         jnp.concatenate(columns, 1),
         precision=lax.Precision.HIGHEST,
         preferred_element_type=f32,
     )
-    for r in range(rows):
+    for r in range(9):
+        line, step = r // 3, r % 3
         for q in range(4):
-            out_ref[pl.ds(r * 4 + q, groups, stride=rows * 4), :] = moved[
-                q * groups : (q + 1) * groups, r * CELLS : (r + 1) * CELLS
-            ]
+            row = step * 2 + q if q < 2 else 6 + (step - 1) * 2 + q - 2
+            if q < 2 or step > 0:
+                out_ref[pl.ds(line * 10 + row, GROUP, stride=30), :] = moved[
+                    q * GROUP : (q + 1) * GROUP, r * CELLS : (r + 1) * CELLS
+                ]
 
 
 def last_kernel(w_ref, in_ref, pos_ref, mom_ref, ns):
     def value(plane, kind, bead):
-        return in_ref[pl.ds(plane * COMP * 4 + kind * 2 + bead, COMP, stride=4), :]
+        half, step = place_of(plane)
+        row = step * 2 + bead if kind == 0 else 6 + (step - 1) * 2 + bead
+        return in_ref[pl.ds(half * 240 + row, COMP, stride=10), :]
 
     ns[EXT * PLANE : EXT * PLANE + 32, :] = jnp.zeros((32, 2 * CELLS), bf16)
     for plane in range(EXT):
@@ -237,14 +260,16 @@
 def body(positions, momenta, offsets, harmonic, cubic):
     shape = jax.ShapeDtypeStruct
     per_plane = 2 * ROWS * DEPTH * 2 * CELLS
-    groups = lax.axis_size("bead")
     doms = lax.axis_size("dom")
     pos = positions.reshape(2 * COMP * OWN, CELLS)
     mom = momenta.reshape(2 * COMP * OWN, CELLS)
-    planes = shape((6 * COMP, CELLS), f32)
-    to_left, to_right = call(pack_kernel, "pack", [VMEM] * 2, [planes] * 2, [], 0, pos, mom)
-    from_left = lax.ppermute(to_right, "dom", [(i, (i + 1) % doms) for i in range(doms)])
-    from_right = lax.ppermute(to_left, "dom", [((i + 1) % doms, i) for i in range(doms)])
+    own = shape((2 * COMP * OWN, CELLS), f32)
+    halo = shape((6 * COMP, CELLS), f32)
+    (pos,) = call(planes_kernel, "planes", [VMEM], [own], [], EARLY, pos)
+    far, near, mom = call(pack_kernel, "pack", [VMEM] * 2, [halo, halo, own], [], EARLY, pos, mom)
+    between = [(i, (i + 1) % doms) for i in range(1, doms, 2)]
+    far = lax.ppermute(far, "dom", between + [(j, i) for i, j in between])
+    near = lax.ppermute(near, "dom", [(i, i ^ 1) for i in range(doms)])
     weights, half = call(
         inner_kernel,
         "inner",
@@ -264,24 +289,19 @@
         pos,
         mom,
     )
-    rows = EXT * COMP // groups
-    exchanged = shape((groups * rows * 4, CELLS), f32)
     (send,) = call(
-        outer_kernel, "outer", [VMEM] * 6, [exchanged], [neighbours(8)], 4 * per_plane,
-        weights, pos, mom, half, from_left, from_right,
-    )
-
-    def swap(x):
-        x = lax.all_to_all(x.reshape(groups, rows, 4, CELLS), "bead", 0, 0, tiled=True)
-        return x.reshape(groups * rows * 4, CELLS)
-
+        outer_kernel, "outer", [VMEM] * 6, [shape((GROUP * 36, CELLS), f32)], [neighbours(8)], 4 * per_plane,
+        weights, pos, mom, half, far, near,
+    )
+    got = lax.all_to_all(send.reshape(GROUP, 9, 4, CELLS), "bead", 0, 0, tiled=True)
     (back,) = call(
-        functools.partial(bead_kernel, groups, rows), "beads", [VMEM] * 2, [exchanged], [],
-        2 * 64 * 64 * 6 * rows * CELLS, jnp.asarray(propagator(groups)), swap(send),
-    )
-    own = shape((2 * COMP * OWN, CELLS), f32)
+        bead_kernel, "beads", [VMEM] * 2, [shape((GROUP * 30, CELLS), f32)], [], 2 * 64 * 64 * 9 * CELLS,
+        jnp.asarray(propagator(GROUP)), got.reshape(GROUP * 36, CELLS),
+    )
+    got = lax.all_to_all(back.reshape(GROUP, 15, 2, CELLS), "bead", 0, 0, tiled=True)
     new_pos, new_mom = call(
-        last_kernel, "last", [VMEM] * 2, [own] * 2, [neighbours(EXT)], 4 * per_plane, weights, swap(back)
+        last_kernel, "last", [VMEM] * 2, [own] * 2, [neighbours(EXT)], 4 * per_plane,
+        weights, got.reshape(GROUP * 30, CELLS),
     )
     return new_pos.reshape(positions.shape), new_mom.reshape(momenta.shape)
 

time: 61.8 us -> 57.4 us (0.929)
  the two profiles are of different devices: /device:TPU:24 before, /device:TPU:2 now
where the time goes in v1:
time: 57.4 us; the launch traced here: 57.1 us
  blocking collectives  36.3 us (63%)
  Pallas kernels  9.82 us (17%)
  starting transfers between devices  8.43 us (15%)
  local copies, waits for them, and re-layouts  1.79 us (3%)
  between operations  0.73 us (1%)
    all_to_all x1, blocking collectives, body(): lax.all_to_all(send.reshape(GROUP, 9, 4, CELLS), 'bead', 0, 0, tiled=True)  22 us
    all_to_all x1, blocking collectives, body(): lax.all_to_all(back.reshape(GROUP, 15, 2, CELLS), 'bead', 0, 0, tiled=True)  14.3 us
    pallas_call x6, Pallas kernels, call(): pl.pallas_call(kernel, name=name, in_specs=ins, out_specs=[VMEM] * len(ou...  9.82 us
    ppermute x1, starting transfers between devices, body(): far = lax.ppermute(far, 'dom', between + [(j, i) for i, j in between])  6.51 us
    ppermute x1, starting transfers between devices, body(): near = lax.ppermute(near, 'dom', [(i, i ^ 1) for i in range(doms)])  1.92 us
    unnamed x12, local copies, waits for them, and re-layouts  1.79 us
  transfers between devices with their start and end apart: 2, of which 0 were waited for; matrix products, arithmetic and copies ran while one was open for 0% of the time, Pallas kernels for 5%

profile of v1, /device:TPU:2, one launch (start us, length us, event | category | flops | bytes accessed | tf_op | source)
XLA Modules:
  0.0 57.1 jit_solution(2257452885491008292)
XLA Ops:
  0.6 0.0 copy-start.2
  0.6 0.9 %copy-done.2 = f32[2,24,4,128]{3,2,1,0:T(4,128)S(1)} copy-done((f32[2,24,4,128]{3,2,1,0:T(4,128)S(1)}, f32[2,24,4,128]{3,2,1,0:T(4,128)}, u32[]{:S(2)}) %copy-start.2) | copy-done | bytes 98328
  1.5 0.0 copy-start.3
  1.5 0.9 %copy-done.3 = f32[2,24,4,128]{3,2,1,0:T(4,128)S(1)} copy-done((f32[2,24,4,128]{3,2,1,0:T(4,128)S(1)}, f32[2,24,4,128]{3,2,1,0:T(4,128)}, u32[]{:S(2)}) %copy-start.3) | copy-done | bytes 98328
  2.4 0.0 copy-start.1
  2.4 0.0 copy-start.4
  2.4 0.0 copy-start.5
  2.5 6.5 %collective-permute-start = (f32[144,128]{1,0:T(8,128)S(1)}, f32[144,128]{1,0:T(8,128)S(1)}, u32[]{:S(2)}, u32[]{:S(2)}) collective-permute-start(f32[144,128]{1,0:T(8,128)S(1)} %get-tuple-element.12), channel_id=1, source_target_pairs={{1,2},{3,4},{5,6},{7,8},{9,10},{11,12},{13,14},{15,16},{17,18},{19... | collective-permute-start | bytes 221192 | tf_op jit(solution)/shard_map/ppermute | solution.py:271
  9.0 1.9 %collective-permute-start.1 = (f32[144,128]{1,0:T(8,128)S(1)}, f32[144,128]{1,0:T(8,128)S(1)}, u32[]{:S(2)}, u32[]{:S(2)}) collective-permute-start(f32[144,128]{1,0:T(8,128)S(1)} %get-tuple-element.13), channel_id=1, source_target_pairs={{0,1},{1,0},{2,3},{3,2},{4,5},{5,4},{6,7},{7,6},{8,9},{9,8},{10,11... | collective-permute-start | bytes 221192 | tf_op jit(solution)/shard_map/ppermute | solution.py:272
  10.9 0.0 copy-done.1
  10.9 0.0 copy-done.4
  10.9 0.0 copy-done.5
  10.9 2.6 %inner.1 = (bf16[608,2048]{1,0:T(8,128)(2,1)S(1)}, f32[48,256]{1,0:T(8,128)S(1)}) custom-call(s32[27]{0:T(128)S(1)} %copy-done.5, f32[24,648]{1,0:T(8,128)S(1)} %copy-done.4, f32[648,576]{1,0:T(8,128)S(1)} %bitcast.13, f32[192,128]{1,0:T(8,128)S(1)} %planes.1.pos_ref, f32[192,128]{1,0:T(8,128)S(1)} %get-tuple-element.9.mom_ref), custom_call_target="tpu_custom_call" | custom-call | flops 1275068416 | bytes 4291436 | tf_op jit(solution)/shard_map/inner/pallas_call | solution.py:244
  13.6 0.0 collective-permute-done.far_ref
  13.6 0.0 collective-permute-done.1.near_ref
  13.6 0.0 copy-start
  13.6 3.1 %outer.1 = f32[576,128]{1,0:T(8,128)S(1)} custom-call(bf16[608,2048]{1,0:T(8,128)(2,1)S(1)} %get-tuple-element.10.w_ref, f32[192,128]{1,0:T(8,128)S(1)} %planes.1.pos_ref, f32[192,128]{1,0:T(8,128)S(1)} %get-tuple-element.9.mom_ref, f32[48,256]{1,0:T(8,128)S(1)} %get-tuple-element.11.half_ref, f32[144,128]{1,0:T(8,128)S(1)} %collective-permute-done.far_ref, ...), custom_call_target="tpu_custom_call" | custom-call | flops 2550136832 | bytes 3178496 | tf_op jit(solution)/shard_map/outer/pallas_call | solution.py:244
  16.7 22.0 %all_to_all.10 = f32[16,9,4,128]{3,2,1,0:T(4,128)S(1)} all-to-all(f32[16,9,4,128]{3,2,1,0:T(4,128)S(1)} %bitcast.11), channel_id=1, replica_groups=mesh['bead'=16,'dom'=32] {'bead'}, dimensions={0} | all-to-all | bytes 589824 | tf_op jit(solution)/shard_map/all_to_all | solution.py:296
  38.7 0.0 copy-done
  38.7 0.4 beads.1
  39.1 14.3 %all_to_all.11 = f32[16,15,2,128]{3,2,1,0:T(2,128)S(1)} all-to-all(f32[16,15,2,128]{3,2,1,0:T(2,128)S(1)} %bitcast.10), channel_id=1, replica_groups=mesh['bead'=16,'dom'=32] {'bead'}, dimensions={0} | all-to-all | bytes 491520 | tf_op jit(solution)/shard_map/all_to_all | solution.py:301
  53.4 3.7 %last.1 = (f32[192,128]{1,0:T(8,128)}, f32[192,128]{1,0:T(8,128)}) custom-call(bf16[608,2048]{1,0:T(8,128)(2,1)S(1)} %get-tuple-element.10.w_ref, f32[480,128]{1,0:T(8,128)S(1)} %bitcast.12), custom_call_target="tpu_custom_call" | custom-call | flops 2550136832 | bytes 2932736 | tf_op jit(solution)/shard_map/last/pallas_call | solution.py:244
  (2 shorter events, 0.0 us)
Async XLA Ops:
  0.6 0.9 %copy-start.2 = (f32[2,24,4,128]{3,2,1,0:T(4,128)S(1)}, f32[2,24,4,128]{3,2,1,0:T(4,128)}, u32[]{:S(2)}) copy-start(f32[2,24,4,128]{3,2,1,0:T(4,128)} %param.6) | copy-start | bytes 294916
  1.5 0.9 %copy-start.3 = (f32[2,24,4,128]{3,2,1,0:T(4,128)S(1)}, f32[2,24,4,128]{3,2,1,0:T(4,128)}, u32[]{:S(2)}) copy-start(f32[2,24,4,128]{3,2,1,0:T(4,128)} %param.7) | copy-start | bytes 294916
  2.4 8.5 %copy-start.1 = (f32[576,648]{0,1:T(8,128)S(1)}, f32[576,648]{0,1:T(8,128)}, u32[]{:S(2)}) copy-start(f32[576,648]{0,1:T(8,128)} %param.10) | copy-start | bytes 4478980
  2.4 8.5 %copy-start.4 = (f32[24,648]{1,0:T(8,128)S(1)}, f32[24,648]{1,0:T(8,128)}, u32[]{:S(2)}) copy-start(f32[24,648]{1,0:T(8,128)} %harm_ref.1) | copy-start | bytes 186628
  2.4 8.5 %copy-start.5 = (s32[27]{0:T(128)S(1)}, s32[27]{0:T(128)}, u32[]{:S(2)}) copy-start(s32[27]{0:T(128)} %off_ref.1) | copy-start | bytes 328
  2.5 11.1 %collective-permute-start = (f32[144,128]{1,0:T(8,128)S(1)}, f32[144,128]{1,0:T(8,128)S(1)}, u32[]{:S(2)}, u32[]{:S(2)}) collective-permute-start(f32[144,128]{1,0:T(8,128)S(1)} %get-tuple-element.12), channel_id=1, source_target_pairs={{1,2},{3,4},{5,6},{7,8},{9,10},{11,12},{13,14},{15,16},{17,18},{19... | collective-permute-start | bytes 221192 | tf_op jit(solution)/shard_map/ppermute | solution.py:271
  9.0 4.6 %collective-permute-start.1 = (f32[144,128]{1,0:T(8,128)S(1)}, f32[144,128]{1,0:T(8,128)S(1)}, u32[]{:S(2)}, u32[]{:S(2)}) collective-permute-start(f32[144,128]{1,0:T(8,128)S(1)} %get-tuple-element.13), channel_id=1, source_target_pairs={{0,1},{1,0},{2,3},{3,2},{4,5},{5,4},{6,7},{7,6},{8,9},{9,8},{10,11... | collective-permute-start | bytes 221192 | tf_op jit(solution)/shard_map/ppermute | solution.py:272
  13.6 25.1 %copy-start = (f32[64,64]{1,0:T(8,128)S(1)}, f32[64,64]{1,0:T(8,128)}, u32[]{:S(2)}) copy-start(f32[64,64]{1,0:T(8,128)} %constant.2.clone.map_ref) | copy-start | bytes 49156

commit v2 on v1

--- a/solution.py
+++ b/solution.py
@@ -23,6 +23,7 @@
 
 EARLY = 10_000_000_000
 GROUP = 16
+HBM = pl.BlockSpec(memory_space=pltpu.HBM)
 SMEM = pl.BlockSpec(memory_space=pltpu.SMEM)
 VMEM = pl.BlockSpec(memory_space=pltpu.VMEM)
 f32 = jnp.float32
@@ -62,7 +63,7 @@
     return whole[np.ix_(order, order)].astype(np.float32)
 
 
-def put_neighbours(ns_ref, slot, bead, field):
+def put_neighbours(ns_ref, row, bead, field):
     z = lax.broadcasted_iota(jnp.int32, field.shape, 1) % CZ
     up = jnp.where(z == CZ - 1, pltpu.roll(field, CZ - 1, 1), pltpu.roll(field, CELLS - 1, 1))
     down = jnp.where(z == 0, pltpu.roll(field, CELLS - CZ + 1, 1), pltpu.roll(field, 1, 1))
@@ -75,13 +76,18 @@
     high = stack.astype(bf16)
     low = (stack - high.astype(f32)).astype(bf16)
     lanes = pl.ds(bead * CELLS, CELLS)
-    ns_ref[pl.ds(slot * PLANE, BLOCK), lanes] = high
-    ns_ref[pl.ds(slot * PLANE + BLOCK, BLOCK), lanes] = low
-    ns_ref[pl.ds(slot * PLANE + 2 * BLOCK, BLOCK), lanes] = high
-
-
-def force_of(w_ref, ns_ref, slot, own):
-    rows = jnp.dot(w_ref[...], ns_ref[pl.ds(slot * PLANE, DEPTH), :], preferred_element_type=f32)
+    ns_ref[pl.ds(row, BLOCK), lanes] = high
+    ns_ref[pl.ds(row + BLOCK, BLOCK), lanes] = low
+    ns_ref[pl.ds(row + 2 * BLOCK, BLOCK), lanes] = high
+
+
+def product(w_ref, first, depth, ns_ref, row):
+    return jnp.dot(
+        w_ref[:, pl.ds(first, depth)], ns_ref[pl.ds(row, depth), :], preferred_element_type=f32
+    )
+
+
+def force_from(rows, own):
     higher = rows[: COMP * COMP].reshape(COMP, COMP, 2 * CELLS)
     anharm = jnp.sum(higher * own[None, :, :], axis=1)
     return -(rows[COMP * COMP : COMP * COMP + COMP] + anharm)
@@ -99,29 +105,45 @@
     return ref[(place * 2 + bead) * COMP : (place * 2 + bead + 1) * COMP, :]
 
 
+def pair(ref, place):
+    return jnp.concatenate([block(ref, place, bead) for bead in range(2)], 1)
+
+
+def clear(ref, row, count):
+    ref[row : row + count, :] = jnp.zeros((count, ref.shape[1]), ref.dtype)
+
+
+def tick_kernel(out_ref):
+    clear(out_ref, 0, 8)
+
+
 def planes_kernel(ref, planes_ref):
     for plane in range(OWN):
         for bead in range(2):
             planes_ref[pl.ds((plane * 2 + bead) * COMP, COMP), :] = own_plane(ref, bead, plane)
 
 
-def pack_kernel(pos_ref, raw_ref, far_ref, near_ref, mom_ref):
+def pack_kernel(blank_ref, raw_pos_ref, raw_mom_ref, far_ref, near_ref, pos_ref, mom_ref):
     core = lax.axis_index("dom") % 2
-    planes_kernel(raw_ref, mom_ref)
+    planes_kernel(raw_pos_ref, pos_ref)
+    planes_kernel(raw_mom_ref, mom_ref)
     for bead in range(2):
-        pos = [block(pos_ref, plane, bead) for plane in range(OWN)]
-        first, last = block(mom_ref, 0, bead), block(mom_ref, OWN - 1, bead)
+        pos = [own_plane(raw_pos_ref, bead, plane) for plane in range(OWN)]
+        first, last = (own_plane(raw_mom_ref, bead, plane) for plane in (0, OWN - 1))
         for place, left, right in ((0, pos[0], pos[2]), (1, pos[1], pos[3]), (2, first, last)):
             rows = pl.ds((place * 2 + bead) * COMP, COMP)
             far_ref[rows, :] = halves(core, left, right)
             near_ref[rows, :] = halves(core, right, left)
 
 
-def inner_kernel(off_ref, harm_ref, cub_ref, pos_ref, mom_ref, w_ref, half_ref, hpad, hturn, wt, cat, ns):
-    ns[OWN * PLANE : OWN * PLANE + 32, :] = jnp.zeros((32, 2 * CELLS), bf16)
+def inner_kernel(
+    off_ref, harm_ref, cub_ref, pos_ref, mom_ref, w_ref, half_ref, side_ref, before_ref, after_ref, hpad, hturn, wt, cat, ns
+):
+    clear(ns, 0, 64)
+    clear(ns, 64 + OWN * PLANE, 96)
     for plane in range(OWN):
         for bead in range(2):
-            put_neighbours(ns, plane, bead, block(pos_ref, plane, bead))
+            put_neighbours(ns, 64 + plane * PLANE, bead, block(pos_ref, plane, bead))
     hpad[...] = jnp.zeros_like(hpad)
     hpad[64 : 64 + COMP, 0 : NOFF * COMP] = harm_ref[...]
     for tile in range(6):
@@ -147,16 +169,21 @@
             turned = cat[k * 128 : (k + 1) * 128, m * 128 : (m + 1) * 128].T
             w_ref[m * 128 : m * 128 + size, k * 128 : (k + 1) * 128] = turned[:size]
     for plane in (1, 2):
-        own = jnp.concatenate([block(pos_ref, plane, bead) for bead in range(2)], 1)
-        mom = jnp.concatenate([block(mom_ref, plane, bead) for bead in range(2)], 1)
-        half_ref[(plane - 1) * COMP : plane * COMP, :] = mom + KICK * force_of(w_ref, ns, plane - 1, own)
+        force = force_from(product(w_ref, 0, DEPTH, ns, 64 + (plane - 1) * PLANE), pair(pos_ref, plane))
+        half_ref[(plane - 1) * COMP : plane * COMP, :] = pair(mom_ref, plane) + KICK * force
+    side_ref[0:COMP, :] = force_from(product(w_ref, 640, 1408, ns, 32), pair(pos_ref, 0))
+    side_ref[COMP:, :] = force_from(product(w_ref, 0, 1408, ns, 64 + 2 * PLANE), pair(pos_ref, OWN - 1))
+    before_ref[...] = product(w_ref, 1280, 768, ns, 0)
+    after_ref[...] = product(w_ref, 0, 768, ns, 64 + 3 * PLANE)
 
 
 def place_of(plane):
     return (0, plane) if plane < 3 else (1, EXT - 1 - plane)
 
 
-def outer_kernel(w_ref, pos_ref, mom_ref, half_ref, far_ref, near_ref, send_ref, ns):
+def outer_kernel(
+    w_ref, pos_ref, mom_ref, half_ref, side_ref, before_ref, after_ref, far_ref, near_ref, send_ref, lower, upper
+):
     core = lax.axis_index("dom") % 2
     left = [[halves(core, block(far_ref, i, bead), block(near_ref, i, bead)) for bead in range(2)] for i in range(3)]
     right = [[halves(core, block(near_ref, i, bead), block(far_ref, i, bead)) for bead in range(2)] for i in range(3)]
@@ -179,10 +206,13 @@
         half, step = place_of(plane + 1)
         send_ref[pl.ds(half * 288 + step * 4 + kind * 2 + bead, COMP, stride=12), :] = value
 
-    ns[8 * PLANE : 8 * PLANE + 32, :] = jnp.zeros((32, 2 * CELLS), bf16)
-    for plane in range(-2, OWN + 2):
-        for bead in range(2):
-            put_neighbours(ns, plane + 2, bead, position(plane, bead))
+    clear(lower, 2 * PLANE, 96)
+    clear(upper, 0, 64)
+    clear(upper, 64 + 2 * PLANE, 32)
+    for i in range(2):
+        for bead in range(2):
+            put_neighbours(lower, i * PLANE, bead, left[i][bead])
+            put_neighbours(upper, 64 + i * PLANE, bead, right[i][bead])
     for plane in range(-1, OWN + 1):
         for bead in range(2):
             store(plane, 0, bead, position(plane, bead))
@@ -191,7 +221,14 @@
             store(plane, 1, bead, half_ref[(plane - 1) * COMP : plane * COMP, bead * CELLS : (bead + 1) * CELLS])
     for plane in (-1, 0, OWN - 1, OWN):
         own = jnp.concatenate([position(plane, bead) for bead in range(2)], 1)
-        force = force_of(w_ref, ns, plane + 1, own)
+        if plane == -1:
+            force = force_from(before_ref[...] + product(w_ref, 0, 1408, lower, 0), own)
+        elif plane == 0:
+            force = side_ref[0:COMP, :] + force_from(product(w_ref, 0, 768, lower, PLANE), own)
+        elif plane == OWN - 1:
+            force = side_ref[COMP:, :] + force_from(product(w_ref, 1280, 768, upper, 0), own)
+        else:
+            force = force_from(after_ref[...] + product(w_ref, 640, 1408, upper, 32), own)
         for bead in range(2):
             half = momentum(plane, bead) + KICK * force[:, bead * CELLS : (bead + 1) * CELLS]
             store(plane, 1, bead, half)
@@ -217,35 +254,41 @@
                 ]
 
 
-def last_kernel(w_ref, in_ref, pos_ref, mom_ref, ns):
+def last_kernel(w_ref, in_ref, pos_hbm, mom_hbm, pos_ref, mom_ref, ns, sem):
     def value(plane, kind, bead):
         half, step = place_of(plane)
         row = step * 2 + bead if kind == 0 else 6 + (step - 1) * 2 + bead
         return in_ref[pl.ds(half * 240 + row, COMP, stride=10), :]
 
-    ns[EXT * PLANE : EXT * PLANE + 32, :] = jnp.zeros((32, 2 * CELLS), bf16)
+    for plane in range(1, OWN + 1):
+        for bead in range(2):
+            pos_ref[pl.ds(bead * COMP * OWN + plane - 1, COMP, stride=OWN), :] = value(plane, 0, bead)
+    out = pltpu.make_async_copy(pos_ref, pos_hbm, sem.at[0])
+    out.start()
+    clear(ns, EXT * PLANE, 32)
     for plane in range(EXT):
         for bead in range(2):
-            field = value(plane, 0, bead)
-            put_neighbours(ns, plane, bead, field)
-            if 1 <= plane <= OWN:
-                pos_ref[pl.ds(bead * COMP * OWN + plane - 1, COMP, stride=OWN), :] = field
+            put_neighbours(ns, plane * PLANE, bead, value(plane, 0, bead))
     for plane in range(1, OWN + 1):
         own = jnp.concatenate([value(plane, 0, bead) for bead in range(2)], 1)
-        force = force_of(w_ref, ns, plane - 1, own)
+        force = force_from(product(w_ref, 0, DEPTH, ns, (plane - 1) * PLANE), own)
         for bead in range(2):
             mom_ref[pl.ds(bead * COMP * OWN + plane - 1, COMP, stride=OWN), :] = (
                 value(plane, 1, bead) + KICK * force[:, bead * CELLS : (bead + 1) * CELLS]
             )
-
-
-def call(kernel, name, ins, outs, scratch, flops, *args):
+    late = pltpu.make_async_copy(mom_ref, mom_hbm, sem.at[1])
+    late.start()
+    out.wait()
+    late.wait()
+
+
+def call(kernel, name, ins, outs, scratch, flops, *args, to=VMEM):
     size = sum(int(np.prod(a.shape)) * a.dtype.itemsize for a in (*args, *outs))
     return pl.pallas_call(
         kernel,
         name=name,
         in_specs=ins,
-        out_specs=[VMEM] * len(outs),
+        out_specs=[to] * len(outs),
         out_shape=list(outs),
         scratch_shapes=scratch,
         compiler_params=pltpu.CompilerParams(vmem_limit_bytes=24 * 1024 * 1024),
@@ -253,8 +296,8 @@
     )(*args)
 
 
-def neighbours(planes):
-    return pltpu.VMEM((planes * PLANE + 32, 2 * CELLS), bf16)
+def neighbours(planes, more):
+    return pltpu.VMEM((planes * PLANE + more, 2 * CELLS), bf16)
 
 
 def body(positions, momenta, offsets, harmonic, cubic):
@@ -265,24 +308,24 @@
     mom = momenta.reshape(2 * COMP * OWN, CELLS)
     own = shape((2 * COMP * OWN, CELLS), f32)
     halo = shape((6 * COMP, CELLS), f32)
-    (pos,) = call(planes_kernel, "planes", [VMEM], [own], [], EARLY, pos)
-    far, near, mom = call(pack_kernel, "pack", [VMEM] * 2, [halo, halo, own], [], EARLY, pos, mom)
+    (blank,) = call(tick_kernel, "blank", [], [shape((8, CELLS), f32)], [], EARLY)
+    far, near, pos, mom = call(pack_kernel, "pack", [VMEM] * 3, [halo, halo, own, own], [], EARLY, blank, pos, mom)
     between = [(i, (i + 1) % doms) for i in range(1, doms, 2)]
     far = lax.ppermute(far, "dom", between + [(j, i) for i, j in between])
     near = lax.ppermute(near, "dom", [(i, i ^ 1) for i in range(doms)])
-    weights, half = call(
+    weights, *parts = call(
         inner_kernel,
         "inner",
         [SMEM] + [VMEM] * 4,
-        [shape((ROWS, DEPTH), bf16), shape((2 * COMP, 2 * CELLS), f32)],
+        [shape((ROWS, DEPTH), bf16)] + [shape((n, 2 * CELLS), f32) for n in (2 * COMP, 2 * COMP, ROWS, ROWS)],
         [
             pltpu.VMEM((128, 768), f32),
             pltpu.VMEM((768, 128), f32),
             pltpu.VMEM((PLANE, 640), f32),
             pltpu.VMEM((DEPTH, 640), bf16),
-            neighbours(OWN),
+            neighbours(OWN, 160),
         ],
-        2 * per_plane,
+        4 * per_plane,
         offsets,
         harmonic,
         cubic.T,
@@ -290,8 +333,8 @@
         mom,
     )
     (send,) = call(
-        outer_kernel, "outer", [VMEM] * 6, [shape((GROUP * 36, CELLS), f32)], [neighbours(8)], 4 * per_plane,
-        weights, pos, mom, half, far, near,
+        outer_kernel, "outer", [VMEM] * 9, [shape((GROUP * 36, CELLS), f32)], [neighbours(2, 96)] * 2, 2 * per_plane,
+        weights, pos, mom, *parts, far, near,
     )
     got = lax.all_to_all(send.reshape(GROUP, 9, 4, CELLS), "bead", 0, 0, tiled=True)
     (back,) = call(
@@ -300,8 +343,9 @@
     )
     got = lax.all_to_all(back.reshape(GROUP, 15, 2, CELLS), "bead", 0, 0, tiled=True)
     new_pos, new_mom = call(
-        last_kernel, "last", [VMEM] * 2, [own] * 2, [neighbours(EXT)], 4 * per_plane,
-        weights, got.reshape(GROUP * 30, CELLS),
+        last_kernel, "last", [VMEM] * 2, [own] * 2,
+        [pltpu.VMEM(own.shape, f32), pltpu.VMEM(own.shape, f32), neighbours(EXT, 32), pltpu.SemaphoreType.DMA((2,))],
+        4 * per_plane, weights, got.reshape(GROUP * 30, CELLS), to=HBM,
     )
     return new_pos.reshape(positions.shape), new_mom.reshape(momenta.shape)
 

time: 57.4 us -> 56.9 us (level)
  local copies, waits for them, and re-layouts: 1.79 us -> 0.93 us
    unnamed x12, local copies, waits for them, and re-layouts: 1.79 us -> 0.93 us
  transfers between devices with their start and end apart: 2 -> 2, of which waited for: 0 -> 0; matrix products, arithmetic and copies ran while one was open for 0% -> 0% of each run, Pallas kernels for 5% -> 7%
where the time goes in v2:
time: 56.9 us; the launch traced here: 56.7 us
  blocking collectives  36.3 us (64%)
  Pallas kernels  10.2 us (18%)
  starting transfers between devices  8.43 us (15%)
  local copies, waits for them, and re-layouts  0.93 us (2%)
  between operations  0.74 us (1%)
    all_to_all x1, blocking collectives, body(): lax.all_to_all(send.reshape(GROUP, 9, 4, CELLS), 'bead', 0, 0, tiled=True)  22 us
    all_to_all x1, blocking collectives, body(): lax.all_to_all(back.reshape(GROUP, 15, 2, CELLS), 'bead', 0, 0, tiled=True)  14.3 us
    pallas_call x6, Pallas kernels, call(): pl.pallas_call(kernel, name=name, in_specs=ins, out_specs=[to] * len(outs...  10.2 us
    ppermute x1, starting transfers between devices, body(): far = lax.ppermute(far, 'dom', between + [(j, i) for i, j in between])  6.51 us
    ppermute x1, starting transfers between devices, body(): near = lax.ppermute(near, 'dom', [(i, i ^ 1) for i in range(doms)])  1.92 us
  transfers between devices with their start and end apart: 2, of which 0 were waited for; matrix products, arithmetic and copies ran while one was open for 0% of the time, Pallas kernels for 7%

profile of v2, /device:TPU:2, one launch (start us, length us, event | category | flops | bytes accessed | tf_op | source)
XLA Modules:
  0.0 56.7 jit_solution(17550727808634092581)
XLA Ops:
  0.6 0.0 copy-start.3
  0.6 0.0 copy-start.2
  0.7 0.9 %copy-done.3 = f32[2,24,4,128]{3,2,1,0:T(4,128)S(1)} copy-done((f32[2,24,4,128]{3,2,1,0:T(4,128)S(1)}, f32[2,24,4,128]{3,2,1,0:T(4,128)}, u32[]{:S(2)}) %copy-start.3) | copy-done | bytes 98328
  1.5 0.0 copy-done.2
  1.6 0.0 copy-start.1
  1.6 0.0 copy-start.4
  1.6 0.0 copy-start.5
  1.6 6.5 %collective-permute-start = (f32[144,128]{1,0:T(8,128)S(1)}, f32[144,128]{1,0:T(8,128)S(1)}, u32[]{:S(2)}, u32[]{:S(2)}) collective-permute-start(f32[144,128]{1,0:T(8,128)S(1)} %get-tuple-element.20), channel_id=1, source_target_pairs={{1,2},{3,4},{5,6},{7,8},{9,10},{11,12},{13,14},{15,16},{17,18},{19... | collective-permute-start | bytes 221192 | tf_op jit(solution)/shard_map/ppermute | solution.py:314
  8.1 1.9 %collective-permute-start.1 = (f32[144,128]{1,0:T(8,128)S(1)}, f32[144,128]{1,0:T(8,128)S(1)}, u32[]{:S(2)}, u32[]{:S(2)}) collective-permute-start(f32[144,128]{1,0:T(8,128)S(1)} %get-tuple-element.21), channel_id=1, source_target_pairs={{0,1},{1,0},{2,3},{3,2},{4,5},{5,4},{6,7},{7,6},{8,9},{9,8},{10,11... | collective-permute-start | bytes 221192 | tf_op jit(solution)/shard_map/ppermute | solution.py:315
  10.1 0.0 copy-done.1
  10.1 0.0 copy-done.4
  10.1 0.0 copy-done.5
  10.1 4.2 %inner.1 = (bf16[608,2048]{1,0:T(8,128)(2,1)S(1)}, f32[48,256]{1,0:T(8,128)S(1)}, f32[48,256]{1,0:T(8,128)S(1)}, f32[608,256]{1,0:T(8,128)S(1)}, f32[608,256]{1,0:T(8,128)S(1)}) custom-call(s32[27]{0:T(128)S(1)} %copy-done.5, f32[24,648]{1,0:T(8,128)S(1)} %copy-done.4, f32[648,576]{1,0:T(8,128)S(1)} %bitcast.13, f32[192,128]{1,0:T(8,128)S(1)} %get-tuple-element.13.pos_ref, ...), custom_call_target="tpu_custom_call" | custom-call | flops 2550136832 | bytes 5585772 | tf_op jit(solution)/shard_map/inner/pallas_call | solution.py:287
  14.3 0.0 collective-permute-done.far_ref
  14.3 0.0 collective-permute-done.1.near_ref
  14.3 0.0 copy-start
  14.3 1.9 %outer.1 = f32[576,128]{1,0:T(8,128)S(1)} custom-call(bf16[608,2048]{1,0:T(8,128)(2,1)S(1)} %get-tuple-element.15.w_ref, f32[192,128]{1,0:T(8,128)S(1)} %get-tuple-element.13.pos_ref, f32[192,128]{1,0:T(8,128)S(1)} %get-tuple-element.14.mom_ref, f32[48,256]{1,0:T(8,128)S(1)} %get-tuple-element.16.half_ref, f32[48,256]{1,0:T(8,128)S(1)} %get-tuple-element.17.side_ref, ...), custom_call_target="tpu_custom_call" | custom-call | flops 1275068416 | bytes 4472832 | tf_op jit(solution)/shard_map/outer/pallas_call | solution.py:287
  16.2 22.0 %all_to_all.10 = f32[16,9,4,128]{3,2,1,0:T(4,128)S(1)} all-to-all(f32[16,9,4,128]{3,2,1,0:T(4,128)S(1)} %bitcast.11), channel_id=1, replica_groups=mesh['bead'=16,'dom'=32] {'bead'}, dimensions={0} | all-to-all | bytes 589824 | tf_op jit(solution)/shard_map/all_to_all | solution.py:339
  38.3 0.0 copy-done
  38.3 0.4 beads.1
  38.6 14.3 %all_to_all.11 = f32[16,15,2,128]{3,2,1,0:T(2,128)S(1)} all-to-all(f32[16,15,2,128]{3,2,1,0:T(2,128)S(1)} %bitcast.10), channel_id=1, replica_groups=mesh['bead'=16,'dom'=32] {'bead'}, dimensions={0} | all-to-all | bytes 491520 | tf_op jit(solution)/shard_map/all_to_all | solution.py:344
  53.0 3.7 %last.1 = (f32[192,128]{1,0:T(8,128)}, f32[192,128]{1,0:T(8,128)}) custom-call(bf16[608,2048]{1,0:T(8,128)(2,1)S(1)} %get-tuple-element.15.w_ref, f32[480,128]{1,0:T(8,128)S(1)} %bitcast.12), custom_call_target="tpu_custom_call" | custom-call | flops 2550136832 | bytes 2932736 | tf_op jit(solution)/shard_map/last/pallas_call | solution.py:287
  (2 shorter events, 0.0 us)
Async XLA Ops:
  0.6 0.9 %copy-start.3 = (f32[2,24,4,128]{3,2,1,0:T(4,128)S(1)}, f32[2,24,4,128]{3,2,1,0:T(4,128)}, u32[]{:S(2)}) copy-start(f32[2,24,4,128]{3,2,1,0:T(4,128)} %param.7) | copy-start | bytes 294916
  0.6 0.9 %copy-start.2 = (f32[2,24,4,128]{3,2,1,0:T(4,128)S(1)}, f32[2,24,4,128]{3,2,1,0:T(4,128)}, u32[]{:S(2)}) copy-start(f32[2,24,4,128]{3,2,1,0:T(4,128)} %param.6) | copy-start | bytes 294916
  1.6 8.5 %copy-start.1 = (f32[576,648]{0,1:T(8,128)S(1)}, f32[576,648]{0,1:T(8,128)}, u32[]{:S(2)}) copy-start(f32[576,648]{0,1:T(8,128)} %param.10) | copy-start | bytes 4478980
  1.6 8.5 %copy-start.4 = (f32[24,648]{1,0:T(8,128)S(1)}, f32[24,648]{1,0:T(8,128)}, u32[]{:S(2)}) copy-start(f32[24,648]{1,0:T(8,128)} %harm_ref.1) | copy-start | bytes 186628
  1.6 8.5 %copy-start.5 = (s32[27]{0:T(128)S(1)}, s32[27]{0:T(128)}, u32[]{:S(2)}) copy-start(s32[27]{0:T(128)} %off_ref.1) | copy-start | bytes 328
  1.6 12.7 %collective-permute-start = (f32[144,128]{1,0:T(8,128)S(1)}, f32[144,128]{1,0:T(8,128)S(1)}, u32[]{:S(2)}, u32[]{:S(2)}) collective-permute-start(f32[144,128]{1,0:T(8,128)S(1)} %get-tuple-element.20), channel_id=1, source_target_pairs={{1,2},{3,4},{5,6},{7,8},{9,10},{11,12},{13,14},{15,16},{17,18},{19... | collective-permute-start | bytes 221192 | tf_op jit(solution)/shard_map/ppermute | solution.py:314
  8.1 6.1 %collective-permute-start.1 = (f32[144,128]{1,0:T(8,128)S(1)}, f32[144,128]{1,0:T(8,128)S(1)}, u32[]{:S(2)}, u32[]{:S(2)}) collective-permute-start(f32[144,128]{1,0:T(8,128)S(1)} %get-tuple-element.21), channel_id=1, source_target_pairs={{0,1},{1,0},{2,3},{3,2},{4,5},{5,4},{6,7},{7,6},{8,9},{9,8},{10,11... | collective-permute-start | bytes 221192 | tf_op jit(solution)/shard_map/ppermute | solution.py:315
  14.3 24.0 %copy-start = (f32[64,64]{1,0:T(8,128)S(1)}, f32[64,64]{1,0:T(8,128)}, u32[]{:S(2)}) copy-start(f32[64,64]{1,0:T(8,128)} %constant.2.clone.map_ref) | copy-start | bytes 49156

commit v3 on v2

--- a/solution.py
+++ b/solution.py
@@ -13,9 +13,10 @@
 CELLS = 128
 OWN = 4
 EXT = OWN + 2
-BLOCK = 224
-PLANE = 3 * BLOCK
-DEPTH = 2048
+NEAR = 9 * COMP
+PART = 256
+POINT = 2 * PART
+QUAD = 4 * POINT
 ROWS = 608
 TIME_STEP = 0.5
 CYCLE_FREQ = 1.0
@@ -71,20 +72,37 @@
     parts = [pltpu.roll(v, CZ, 1) for v in along_z]
     parts += along_z
     parts += [pltpu.roll(v, CELLS - CZ, 1) for v in along_z]
-    parts.append(jnp.zeros((BLOCK - 9 * COMP, CELLS), f32))
+    parts.append(jnp.zeros((PART - NEAR, CELLS), f32))
     stack = jnp.concatenate(parts, 0)
     high = stack.astype(bf16)
     low = (stack - high.astype(f32)).astype(bf16)
     lanes = pl.ds(bead * CELLS, CELLS)
-    ns_ref[pl.ds(row, BLOCK), lanes] = high
-    ns_ref[pl.ds(row + BLOCK, BLOCK), lanes] = low
-    ns_ref[pl.ds(row + 2 * BLOCK, BLOCK), lanes] = high
-
-
-def product(w_ref, first, depth, ns_ref, row):
-    return jnp.dot(
-        w_ref[:, pl.ds(first, depth)], ns_ref[pl.ds(row, depth), :], preferred_element_type=f32
-    )
+    ns_ref[pl.ds(row, PART), lanes] = low
+    ns_ref[pl.ds(row + PART, PART), lanes] = high
+
+
+def put_quad(ns_ref, row, fields):
+    for bead in range(2):
+        d0, d1, d2, d3 = (plane[bead] for plane in fields)
+        for q, field in enumerate((d0 - d2, d1 + d2, d2 - d1, d1 - d3)):
+            put_neighbours(ns_ref, row + q * POINT, bead, field)
+
+
+def two_rows(w_ref, ns_ref, row):
+    m = []
+    for q in range(4):
+        high = jnp.dot(
+            w_ref[:, q * POINT : q * POINT + PART],
+            ns_ref[pl.ds(row + q * POINT + PART, PART), :],
+            preferred_element_type=f32,
+        )
+        rest = jnp.dot(
+            w_ref[:, q * POINT : (q + 1) * POINT],
+            ns_ref[pl.ds(row + q * POINT, POINT), :],
+            preferred_element_type=f32,
+        )
+        m.append(high + rest)
+    return m[0] + (m[1] + m[2]), (m[1] - m[2]) - m[3]
 
 
 def force_from(rows, own):
@@ -136,54 +154,38 @@
             near_ref[rows, :] = halves(core, right, left)
 
 
-def inner_kernel(
-    off_ref, harm_ref, cub_ref, pos_ref, mom_ref, w_ref, half_ref, side_ref, before_ref, after_ref, hpad, hturn, wt, cat, ns
-):
-    clear(ns, 0, 64)
-    clear(ns, 64 + OWN * PLANE, 96)
-    for plane in range(OWN):
-        for bead in range(2):
-            put_neighbours(ns, 64 + plane * PLANE, bead, block(pos_ref, plane, bead))
+def inner_kernel(off_ref, harm_ref, cub_ref, pos_ref, mom_ref, w_ref, half_ref, hpad, hturn, wt, cat, ns):
+    put_quad(ns, 0, [[block(pos_ref, plane, bead) for bead in range(2)] for plane in range(OWN)])
     hpad[...] = jnp.zeros_like(hpad)
     hpad[64 : 64 + COMP, 0 : NOFF * COMP] = harm_ref[...]
     for tile in range(6):
         hturn[tile * 128 : (tile + 1) * 128, :] = hpad[:, tile * 128 : (tile + 1) * 128].T
-    for dx in range(3):
-        wt[dx * BLOCK + 9 * COMP : (dx + 1) * BLOCK, :] = jnp.zeros((8, 640), f32)
     for o in range(NOFF):
-        code = off_ref[o]
-        rows = pl.ds(pl.multiple_of(code * COMP + (code // 9) * 8, 8), COMP)
+        rows = pl.ds(pl.multiple_of(off_ref[o] * COMP, 8), COMP)
         wt[rows, 512:640] = hturn[o * COMP : (o + 1) * COMP, :]
         wt[rows, 0 : COMP * COMP] = cub_ref[o * COMP : (o + 1) * COMP, :]
-    for dx in range(3):
-        rows = wt[dx * BLOCK : (dx + 1) * BLOCK, :]
-        high = rows.astype(bf16)
-        low = (rows - high.astype(f32)).astype(bf16)
-        cat[dx * PLANE : dx * PLANE + BLOCK, :] = high
-        cat[dx * PLANE + BLOCK : dx * PLANE + 2 * BLOCK, :] = high
-        cat[dx * PLANE + 2 * BLOCK : (dx + 1) * PLANE, :] = low
-    cat[3 * PLANE : DEPTH, :] = jnp.zeros((DEPTH - 3 * PLANE, 640), bf16)
+    before, here, after = (wt[dx * NEAR : (dx + 1) * NEAR, :] for dx in range(3))
+    outer = before + after
+    for q, weight in enumerate((before, 0.5 * (outer + here), 0.5 * (outer - here), after)):
+        weight = jnp.concatenate([weight, jnp.zeros((PART - NEAR, 640), f32)], 0)
+        high = weight.astype(bf16)
+        cat[q * POINT : q * POINT + PART, :] = high
+        cat[q * POINT + PART : (q + 1) * POINT, :] = (weight - high.astype(f32)).astype(bf16)
     for m in range(5):
         size = min(128, ROWS - m * 128)
-        for k in range(DEPTH // 128):
+        for k in range(QUAD // 128):
             turned = cat[k * 128 : (k + 1) * 128, m * 128 : (m + 1) * 128].T
             w_ref[m * 128 : m * 128 + size, k * 128 : (k + 1) * 128] = turned[:size]
-    for plane in (1, 2):
-        force = force_from(product(w_ref, 0, DEPTH, ns, 64 + (plane - 1) * PLANE), pair(pos_ref, plane))
+    for plane, rows in zip((1, 2), two_rows(w_ref, ns, 0)):
+        force = force_from(rows, pair(pos_ref, plane))
         half_ref[(plane - 1) * COMP : plane * COMP, :] = pair(mom_ref, plane) + KICK * force
-    side_ref[0:COMP, :] = force_from(product(w_ref, 640, 1408, ns, 32), pair(pos_ref, 0))
-    side_ref[COMP:, :] = force_from(product(w_ref, 0, 1408, ns, 64 + 2 * PLANE), pair(pos_ref, OWN - 1))
-    before_ref[...] = product(w_ref, 1280, 768, ns, 0)
-    after_ref[...] = product(w_ref, 0, 768, ns, 64 + 3 * PLANE)
 
 
 def place_of(plane):
     return (0, plane) if plane < 3 else (1, EXT - 1 - plane)
 
 
-def outer_kernel(
-    w_ref, pos_ref, mom_ref, half_ref, side_ref, before_ref, after_ref, far_ref, near_ref, send_ref, lower, upper
-):
+def outer_kernel(w_ref, pos_ref, mom_ref, half_ref, far_ref, near_ref, send_ref, ns):
     core = lax.axis_index("dom") % 2
     left = [[halves(core, block(far_ref, i, bead), block(near_ref, i, bead)) for bead in range(2)] for i in range(3)]
     right = [[halves(core, block(near_ref, i, bead), block(far_ref, i, bead)) for bead in range(2)] for i in range(3)]
@@ -206,32 +208,20 @@
         half, step = place_of(plane + 1)
         send_ref[pl.ds(half * 288 + step * 4 + kind * 2 + bead, COMP, stride=12), :] = value
 
-    clear(lower, 2 * PLANE, 96)
-    clear(upper, 0, 64)
-    clear(upper, 64 + 2 * PLANE, 32)
-    for i in range(2):
-        for bead in range(2):
-            put_neighbours(lower, i * PLANE, bead, left[i][bead])
-            put_neighbours(upper, 64 + i * PLANE, bead, right[i][bead])
+    for i, first in enumerate((-1, OWN - 1)):
+        put_quad(ns, i * QUAD, [[position(first + n, bead) for bead in range(2)] for n in range(-1, 3)])
     for plane in range(-1, OWN + 1):
         for bead in range(2):
             store(plane, 0, bead, position(plane, bead))
     for plane in (1, 2):
         for bead in range(2):
             store(plane, 1, bead, half_ref[(plane - 1) * COMP : plane * COMP, bead * CELLS : (bead + 1) * CELLS])
-    for plane in (-1, 0, OWN - 1, OWN):
-        own = jnp.concatenate([position(plane, bead) for bead in range(2)], 1)
-        if plane == -1:
-            force = force_from(before_ref[...] + product(w_ref, 0, 1408, lower, 0), own)
-        elif plane == 0:
-            force = side_ref[0:COMP, :] + force_from(product(w_ref, 0, 768, lower, PLANE), own)
-        elif plane == OWN - 1:
-            force = side_ref[COMP:, :] + force_from(product(w_ref, 1280, 768, upper, 0), own)
-        else:
-            force = force_from(after_ref[...] + product(w_ref, 640, 1408, upper, 32), own)
-        for bead in range(2):
-            half = momentum(plane, bead) + KICK * force[:, bead * CELLS : (bead + 1) * CELLS]
-            store(plane, 1, bead, half)
+    for i, first in enumerate((-1, OWN - 1)):
+        for plane, rows in zip((first, first + 1), two_rows(w_ref, ns, i * QUAD)):
+            force = force_from(rows, jnp.concatenate([position(plane, bead) for bead in range(2)], 1))
+            for bead in range(2):
+                half = momentum(plane, bead) + KICK * force[:, bead * CELLS : (bead + 1) * CELLS]
+                store(plane, 1, bead, half)
 
 
 def bead_kernel(map_ref, in_ref, out_ref):
@@ -265,17 +255,15 @@
             pos_ref[pl.ds(bead * COMP * OWN + plane - 1, COMP, stride=OWN), :] = value(plane, 0, bead)
     out = pltpu.make_async_copy(pos_ref, pos_hbm, sem.at[0])
     out.start()
-    clear(ns, EXT * PLANE, 32)
-    for plane in range(EXT):
-        for bead in range(2):
-            put_neighbours(ns, plane * PLANE, bead, value(plane, 0, bead))
-    for plane in range(1, OWN + 1):
-        own = jnp.concatenate([value(plane, 0, bead) for bead in range(2)], 1)
-        force = force_from(product(w_ref, 0, DEPTH, ns, (plane - 1) * PLANE), own)
-        for bead in range(2):
-            mom_ref[pl.ds(bead * COMP * OWN + plane - 1, COMP, stride=OWN), :] = (
-                value(plane, 1, bead) + KICK * force[:, bead * CELLS : (bead + 1) * CELLS]
-            )
+    for i, first in enumerate((1, 3)):
+        put_quad(ns, i * QUAD, [[value(first + n, 0, bead) for bead in range(2)] for n in range(-1, 3)])
+    for i, first in enumerate((1, 3)):
+        for plane, rows in zip((first, first + 1), two_rows(w_ref, ns, i * QUAD)):
+            force = force_from(rows, jnp.concatenate([value(plane, 0, bead) for bead in range(2)], 1))
+            for bead in range(2):
+                mom_ref[pl.ds(bead * COMP * OWN + plane - 1, COMP, stride=OWN), :] = (
+                    value(plane, 1, bead) + KICK * force[:, bead * CELLS : (bead + 1) * CELLS]
+                )
     late = pltpu.make_async_copy(mom_ref, mom_hbm, sem.at[1])
     late.start()
     out.wait()
@@ -296,13 +284,13 @@
     )(*args)
 
 
-def neighbours(planes, more):
-    return pltpu.VMEM((planes * PLANE + more, 2 * CELLS), bf16)
+def neighbours(quads):
+    return pltpu.VMEM((quads * QUAD, 2 * CELLS), bf16)
 
 
 def body(positions, momenta, offsets, harmonic, cubic):
     shape = jax.ShapeDtypeStruct
-    per_plane = 2 * ROWS * DEPTH * 2 * CELLS
+    per_plane = 2 * ROWS * (QUAD * 3 // 4) * 2 * CELLS
     doms = lax.axis_size("dom")
     pos = positions.reshape(2 * COMP * OWN, CELLS)
     mom = momenta.reshape(2 * COMP * OWN, CELLS)
@@ -313,19 +301,19 @@
     between = [(i, (i + 1) % doms) for i in range(1, doms, 2)]
     far = lax.ppermute(far, "dom", between + [(j, i) for i, j in between])
     near = lax.ppermute(near, "dom", [(i, i ^ 1) for i in range(doms)])
-    weights, *parts = call(
+    weights, half = call(
         inner_kernel,
         "inner",
         [SMEM] + [VMEM] * 4,
-        [shape((ROWS, DEPTH), bf16)] + [shape((n, 2 * CELLS), f32) for n in (2 * COMP, 2 * COMP, ROWS, ROWS)],
+        [shape((ROWS, QUAD), bf16), shape((2 * COMP, 2 * CELLS), f32)],
         [
             pltpu.VMEM((128, 768), f32),
             pltpu.VMEM((768, 128), f32),
-            pltpu.VMEM((PLANE, 640), f32),
-            pltpu.VMEM((DEPTH, 640), bf16),
-            neighbours(OWN, 160),
+            pltpu.VMEM((3 * NEAR, 640), f32),
+            pltpu.VMEM((QUAD, 640), bf16),
+            neighbours(1),
         ],
-        4 * per_plane,
+        2 * per_plane,
         offsets,
         harmonic,
         cubic.T,
@@ -333,8 +321,8 @@
         mom,
     )
     (send,) = call(
-        outer_kernel, "outer", [VMEM] * 9, [shape((GROUP * 36, CELLS), f32)], [neighbours(2, 96)] * 2, 2 * per_plane,
-        weights, pos, mom, *parts, far, near,
+        outer_kernel, "outer", [VMEM] * 6, [shape((GROUP * 36, CELLS), f32)], [neighbours(2)], 4 * per_plane,
+        weights, pos, mom, half, far, near,
     )
     got = lax.all_to_all(send.reshape(GROUP, 9, 4, CELLS), "bead", 0, 0, tiled=True)
     (back,) = call(
@@ -344,7 +332,7 @@
     got = lax.all_to_all(back.reshape(GROUP, 15, 2, CELLS), "bead", 0, 0, tiled=True)
     new_pos, new_mom = call(
         last_kernel, "last", [VMEM] * 2, [own] * 2,
-        [pltpu.VMEM(own.shape, f32), pltpu.VMEM(own.shape, f32), neighbours(EXT, 32), pltpu.SemaphoreType.DMA((2,))],
+        [pltpu.VMEM(own.shape, f32), pltpu.VMEM(own.shape, f32), neighbours(2), pltpu.SemaphoreType.DMA((2,))],
         4 * per_plane, weights, got.reshape(GROUP * 30, CELLS), to=HBM,
     )
     return new_pos.reshape(positions.shape), new_mom.reshape(momenta.shape)

time: 56.9 us -> 55.9 us (0.982)
  Pallas kernels: 10.2 us -> 9.18 us
    pallas_call x6, Pallas kernels: 10.2 us -> 9.18 us  [call(): pl.pallas_call(kernel, name=name, in_specs=ins, out_specs=[to] * len(outs...]
  transfers between devices with their start and end apart: 2 -> 2, of which waited for: 0 -> 0; matrix products, arithmetic and copies ran while one was open for 0% -> 0% of each run, Pallas kernels for 7% -> 5%
where the time goes in v3:
time: 55.9 us; the launch traced here: 55.6 us
  blocking collectives  36.3 us (65%)
  Pallas kernels  9.18 us (16%)
  starting transfers between devices  8.43 us (15%)
  local copies, waits for them, and re-layouts  0.93 us (2%)
  between operations  0.75 us (1%)
    all_to_all x1, blocking collectives, body(): lax.all_to_all(send.reshape(GROUP, 9, 4, CELLS), 'bead', 0, 0, tiled=True)  22 us
    all_to_all x1, blocking collectives, body(): lax.all_to_all(back.reshape(GROUP, 15, 2, CELLS), 'bead', 0, 0, tiled=True)  14.3 us
    pallas_call x6, Pallas kernels, call(): pl.pallas_call(kernel, name=name, in_specs=ins, out_specs=[to] * len(outs...  9.18 us
    ppermute x1, starting transfers between devices, body(): far = lax.ppermute(far, 'dom', between + [(j, i) for i, j in between])  6.51 us
    ppermute x1, starting transfers between devices, body(): near = lax.ppermute(near, 'dom', [(i, i ^ 1) for i in range(doms)])  1.92 us
  transfers between devices with their start and end apart: 2, of which 0 were waited for; matrix products, arithmetic and copies ran while one was open for 0% of the time, Pallas kernels for 5%

profile of v3, /device:TPU:2, one launch (start us, length us, event | category | flops | bytes accessed | tf_op | source)
XLA Modules:
  0.0 55.6 jit_solution(10464911733056820782)
XLA Ops:
  0.6 0.0 copy-start.3
  0.6 0.0 copy-start.2
  0.7 0.9 %copy-done.3 = f32[2,24,4,128]{3,2,1,0:T(4,128)S(1)} copy-done((f32[2,24,4,128]{3,2,1,0:T(4,128)S(1)}, f32[2,24,4,128]{3,2,1,0:T(4,128)}, u32[]{:S(2)}) %copy-start.3) | copy-done | bytes 98328
  1.5 0.0 copy-done.2
  1.6 0.0 copy-start.1
  1.6 0.0 copy-start.4
  1.6 0.0 copy-start.5
  1.6 6.5 %collective-permute-start = (f32[144,128]{1,0:T(8,128)S(1)}, f32[144,128]{1,0:T(8,128)S(1)}, u32[]{:S(2)}, u32[]{:S(2)}) collective-permute-start(f32[144,128]{1,0:T(8,128)S(1)} %get-tuple-element.14), channel_id=1, source_target_pairs={{1,2},{3,4},{5,6},{7,8},{9,10},{11,12},{13,14},{15,16},{17,18},{19... | collective-permute-start | bytes 221192 | tf_op jit(solution)/shard_map/ppermute | solution.py:302
  8.1 1.9 %collective-permute-start.1 = (f32[144,128]{1,0:T(8,128)S(1)}, f32[144,128]{1,0:T(8,128)S(1)}, u32[]{:S(2)}, u32[]{:S(2)}) collective-permute-start(f32[144,128]{1,0:T(8,128)S(1)} %get-tuple-element.15), channel_id=1, source_target_pairs={{0,1},{1,0},{2,3},{3,2},{4,5},{5,4},{6,7},{7,6},{8,9},{9,8},{10,11... | collective-permute-start | bytes 221192 | tf_op jit(solution)/shard_map/ppermute | solution.py:303
  10.1 0.0 copy-done.1
  10.1 0.0 copy-done.4
  10.1 0.0 copy-done.5
  10.1 2.9 %inner.1 = (bf16[608,2048]{1,0:T(8,128)(2,1)S(1)}, f32[48,256]{1,0:T(8,128)S(1)}) custom-call(s32[27]{0:T(128)S(1)} %copy-done.5, f32[24,648]{1,0:T(8,128)S(1)} %copy-done.4, f32[648,576]{1,0:T(8,128)S(1)} %bitcast.13, f32[192,128]{1,0:T(8,128)S(1)} %get-tuple-element.10.pos_ref, f32[192,128]{1,0:T(8,128)S(1)} %get-tuple-element.11.mom_ref), custom_call_target="tpu_custom_call" | custom-call | flops 956301312 | bytes 4291436 | tf_op jit(solution)/shard_map/inner/pallas_call | solution.py:275
  13.0 0.0 collective-permute-done.far_ref
  13.0 0.0 collective-permute-done.1.near_ref
  13.0 0.0 copy-start
  13.0 2.6 %outer.1 = f32[576,128]{1,0:T(8,128)S(1)} custom-call(bf16[608,2048]{1,0:T(8,128)(2,1)S(1)} %get-tuple-element.12.w_ref, f32[192,128]{1,0:T(8,128)S(1)} %get-tuple-element.10.pos_ref, f32[192,128]{1,0:T(8,128)S(1)} %get-tuple-element.11.mom_ref, f32[48,256]{1,0:T(8,128)S(1)} %get-tuple-element.13.half_ref, f32[144,128]{1,0:T(8,128)S(1)} %collective-permute-done.far_ref, ...), custom_call_target="tpu_custom_call" | custom-call | flops 1912602624 | bytes 3178496 | tf_op jit(solution)/shard_map/outer/pallas_call | solution.py:275
  15.6 22.0 %all_to_all.10 = f32[16,9,4,128]{3,2,1,0:T(4,128)S(1)} all-to-all(f32[16,9,4,128]{3,2,1,0:T(4,128)S(1)} %bitcast.11), channel_id=1, replica_groups=mesh['bead'=16,'dom'=32] {'bead'}, dimensions={0} | all-to-all | bytes 589824 | tf_op jit(solution)/shard_map/all_to_all | solution.py:327
  37.6 0.0 copy-done
  37.6 0.4 beads.1
  38.0 14.3 %all_to_all.11 = f32[16,15,2,128]{3,2,1,0:T(2,128)S(1)} all-to-all(f32[16,15,2,128]{3,2,1,0:T(2,128)S(1)} %bitcast.10), channel_id=1, replica_groups=mesh['bead'=16,'dom'=32] {'bead'}, dimensions={0} | all-to-all | bytes 491520 | tf_op jit(solution)/shard_map/all_to_all | solution.py:332
  52.3 3.3 %last.1 = (f32[192,128]{1,0:T(8,128)}, f32[192,128]{1,0:T(8,128)}) custom-call(bf16[608,2048]{1,0:T(8,128)(2,1)S(1)} %get-tuple-element.12.w_ref, f32[480,128]{1,0:T(8,128)S(1)} %bitcast.12), custom_call_target="tpu_custom_call" | custom-call | flops 1912602624 | bytes 2932736 | tf_op jit(solution)/shard_map/last/pallas_call | solution.py:275
  (2 shorter events, 0.0 us)
Async XLA Ops:
  0.6 0.9 %copy-start.3 = (f32[2,24,4,128]{3,2,1,0:T(4,128)S(1)}, f32[2,24,4,128]{3,2,1,0:T(4,128)}, u32[]{:S(2)}) copy-start(f32[2,24,4,128]{3,2,1,0:T(4,128)} %param.7) | copy-start | bytes 294916
  0.6 0.9 %copy-start.2 = (f32[2,24,4,128]{3,2,1,0:T(4,128)S(1)}, f32[2,24,4,128]{3,2,1,0:T(4,128)}, u32[]{:S(2)}) copy-start(f32[2,24,4,128]{3,2,1,0:T(4,128)} %param.6) | copy-start | bytes 294916
  1.6 8.5 %copy-start.1 = (f32[576,648]{0,1:T(8,128)S(1)}, f32[576,648]{0,1:T(8,128)}, u32[]{:S(2)}) copy-start(f32[576,648]{0,1:T(8,128)} %param.10) | copy-start | bytes 4478980
  1.6 8.5 %copy-start.4 = (f32[24,648]{1,0:T(8,128)S(1)}, f32[24,648]{1,0:T(8,128)}, u32[]{:S(2)}) copy-start(f32[24,648]{1,0:T(8,128)} %harm_ref.1) | copy-start | bytes 186628
  1.6 8.5 %copy-start.5 = (s32[27]{0:T(128)S(1)}, s32[27]{0:T(128)}, u32[]{:S(2)}) copy-start(s32[27]{0:T(128)} %off_ref.1) | copy-start | bytes 328
  1.6 11.3 %collective-permute-start = (f32[144,128]{1,0:T(8,128)S(1)}, f32[144,128]{1,0:T(8,128)S(1)}, u32[]{:S(2)}, u32[]{:S(2)}) collective-permute-start(f32[144,128]{1,0:T(8,128)S(1)} %get-tuple-element.14), channel_id=1, source_target_pairs={{1,2},{3,4},{5,6},{7,8},{9,10},{11,12},{13,14},{15,16},{17,18},{19... | collective-permute-start | bytes 221192 | tf_op jit(solution)/shard_map/ppermute | solution.py:302
  8.1 4.8 %collective-permute-start.1 = (f32[144,128]{1,0:T(8,128)S(1)}, f32[144,128]{1,0:T(8,128)S(1)}, u32[]{:S(2)}, u32[]{:S(2)}) collective-permute-start(f32[144,128]{1,0:T(8,128)S(1)} %get-tuple-element.15), channel_id=1, source_target_pairs={{0,1},{1,0},{2,3},{3,2},{4,5},{5,4},{6,7},{7,6},{8,9},{9,8},{10,11... | collective-permute-start | bytes 221192 | tf_op jit(solution)/shard_map/ppermute | solution.py:303
  13.0 24.6 %copy-start = (f32[64,64]{1,0:T(8,128)S(1)}, f32[64,64]{1,0:T(8,128)}, u32[]{:S(2)}) copy-start(f32[64,64]{1,0:T(8,128)} %constant.2.clone.map_ref) | copy-start | bytes 49156

commit v4 on v3

--- a/solution.py
+++ b/solution.py
@@ -154,28 +154,40 @@
             near_ref[rows, :] = halves(core, right, left)
 
 
-def inner_kernel(off_ref, harm_ref, cub_ref, pos_ref, mom_ref, w_ref, half_ref, hpad, hturn, wt, cat, ns):
+def inner_kernel(off_ref, harm_ref, cub_ref, pos_ref, mom_ref, w_ref, half_ref, order, hpad, tail, cat, ns):
     put_quad(ns, 0, [[block(pos_ref, plane, bead) for bead in range(2)] for plane in range(OWN)])
-    hpad[...] = jnp.zeros_like(hpad)
+    for o in range(NOFF):
+        order[o] = 0
+    for o in range(NOFF):
+        order[off_ref[o]] = o
+    clear(hpad, 0, 128)
     hpad[64 : 64 + COMP, 0 : NOFF * COMP] = harm_ref[...]
     for tile in range(6):
-        hturn[tile * 128 : (tile + 1) * 128, :] = hpad[:, tile * 128 : (tile + 1) * 128].T
-    for o in range(NOFF):
-        rows = pl.ds(pl.multiple_of(off_ref[o] * COMP, 8), COMP)
-        wt[rows, 512:640] = hturn[o * COMP : (o + 1) * COMP, :]
-        wt[rows, 0 : COMP * COMP] = cub_ref[o * COMP : (o + 1) * COMP, :]
-    before, here, after = (wt[dx * NEAR : (dx + 1) * NEAR, :] for dx in range(3))
-    outer = before + after
-    for q, weight in enumerate((before, 0.5 * (outer + here), 0.5 * (outer - here), after)):
-        weight = jnp.concatenate([weight, jnp.zeros((PART - NEAR, 640), f32)], 0)
-        high = weight.astype(bf16)
-        cat[q * POINT : q * POINT + PART, :] = high
-        cat[q * POINT + PART : (q + 1) * POINT, :] = (weight - high.astype(f32)).astype(bf16)
-    for m in range(5):
-        size = min(128, ROWS - m * 128)
-        for k in range(QUAD // 128):
-            turned = cat[k * 128 : (k + 1) * 128, m * 128 : (m + 1) * 128].T
-            w_ref[m * 128 : m * 128 + size, k * 128 : (k + 1) * 128] = turned[:size]
+        tail[tile * 128 : (tile + 1) * 128, :] = hpad[:, tile * 128 : (tile + 1) * 128].T
+    tail[0 : NOFF * COMP, 0:64] = cub_ref[:, 512 : COMP * COMP]
+
+    def weights_of(code):
+        rows = pl.ds(pl.multiple_of(order[code] * COMP, 8), COMP)
+        return jnp.concatenate([cub_ref[rows, 0:512], tail[rows, :]], 1)
+
+    for s in range(0, 9, 2):
+        shifts = range(s, min(s + 2, 9))
+        before, here, after = (
+            jnp.concatenate([weights_of(dx * 9 + shift) for shift in shifts], 0) for dx in range(3)
+        )
+        outer = before + after
+        for q, weight in enumerate((before, 0.5 * (outer + here), 0.5 * (outer - here), after)):
+            if len(shifts) == 1:
+                weight = jnp.concatenate([weight, jnp.zeros((PART - NEAR, 640), f32)], 0)
+            high = weight.astype(bf16)
+            rows = pl.ds(q * POINT + s * COMP, weight.shape[0])
+            cat[rows, :] = high
+            rows = pl.ds(q * POINT + PART + s * COMP, weight.shape[0])
+            cat[rows, :] = (weight - high.astype(f32)).astype(bf16)
+    for m in range(0, ROWS, 128):
+        size = min(128, ROWS - m)
+        for k in range(0, QUAD, 128):
+            w_ref[m : m + size, k : k + 128] = cat[k : k + 128, m : m + 128].T[:size]
     for plane, rows in zip((1, 2), two_rows(w_ref, ns, 0)):
         force = force_from(rows, pair(pos_ref, plane))
         half_ref[(plane - 1) * COMP : plane * COMP, :] = pair(mom_ref, plane) + KICK * force
@@ -307,9 +319,9 @@
         [SMEM] + [VMEM] * 4,
         [shape((ROWS, QUAD), bf16), shape((2 * COMP, 2 * CELLS), f32)],
         [
+            pltpu.SMEM((NOFF,), jnp.int32),
             pltpu.VMEM((128, 768), f32),
             pltpu.VMEM((768, 128), f32),
-            pltpu.VMEM((3 * NEAR, 640), f32),
             pltpu.VMEM((QUAD, 640), bf16),
             neighbours(1),
         ],

time: 55.9 us -> 55.7 us (level)
  no operation moved by 1% of the time
where the time goes in v4:
time: 55.7 us; the launch traced here: 55.5 us
  blocking collectives  36.3 us (65%)
  Pallas kernels  9.03 us (16%)
  starting transfers between devices  8.43 us (15%)
  local copies, waits for them, and re-layouts  0.93 us (2%)
  between operations  0.74 us (1%)
    all_to_all x1, blocking collectives, body(): lax.all_to_all(send.reshape(GROUP, 9, 4, CELLS), 'bead', 0, 0, tiled=True)  22 us
    all_to_all x1, blocking collectives, body(): lax.all_to_all(back.reshape(GROUP, 15, 2, CELLS), 'bead', 0, 0, tiled=True)  14.3 us
    pallas_call x6, Pallas kernels, call(): pl.pallas_call(kernel, name=name, in_specs=ins, out_specs=[to] * len(outs...  9.03 us
    ppermute x1, starting transfers between devices, body(): far = lax.ppermute(far, 'dom', between + [(j, i) for i, j in between])  6.51 us
    ppermute x1, starting transfers between devices, body(): near = lax.ppermute(near, 'dom', [(i, i ^ 1) for i in range(doms)])  1.92 us
  transfers between devices with their start and end apart: 2, of which 0 were waited for; matrix products, arithmetic and copies ran while one was open for 0% of the time, Pallas kernels for 5%

profile of v4, /device:TPU:2, one launch (start us, length us, event | category | flops | bytes accessed | tf_op | source)
XLA Modules:
  0.0 55.5 jit_solution(1990627294342033823)
XLA Ops:
  0.6 0.0 copy-start.3
  0.6 0.0 copy-start.2
  0.7 0.9 %copy-done.3 = f32[2,24,4,128]{3,2,1,0:T(4,128)S(1)} copy-done((f32[2,24,4,128]{3,2,1,0:T(4,128)S(1)}, f32[2,24,4,128]{3,2,1,0:T(4,128)}, u32[]{:S(2)}) %copy-start.3) | copy-done | bytes 98328
  1.5 0.0 copy-done.2
  1.6 0.0 copy-start.1
  1.6 0.0 copy-start.4
  1.6 0.0 copy-start.5
  1.6 6.5 %collective-permute-start = (f32[144,128]{1,0:T(8,128)S(1)}, f32[144,128]{1,0:T(8,128)S(1)}, u32[]{:S(2)}, u32[]{:S(2)}) collective-permute-start(f32[144,128]{1,0:T(8,128)S(1)} %get-tuple-element.14), channel_id=1, source_target_pairs={{1,2},{3,4},{5,6},{7,8},{9,10},{11,12},{13,14},{15,16},{17,18},{19... | collective-permute-start | bytes 221192 | tf_op jit(solution)/shard_map/ppermute | solution.py:314
  8.1 1.9 %collective-permute-start.1 = (f32[144,128]{1,0:T(8,128)S(1)}, f32[144,128]{1,0:T(8,128)S(1)}, u32[]{:S(2)}, u32[]{:S(2)}) collective-permute-start(f32[144,128]{1,0:T(8,128)S(1)} %get-tuple-element.15), channel_id=1, source_target_pairs={{0,1},{1,0},{2,3},{3,2},{4,5},{5,4},{6,7},{7,6},{8,9},{9,8},{10,11... | collective-permute-start | bytes 221192 | tf_op jit(solution)/shard_map/ppermute | solution.py:315
  10.1 0.0 copy-done.1
  10.1 0.0 copy-done.4
  10.1 0.0 copy-done.5
  10.1 2.7 %inner.1 = (bf16[608,2048]{1,0:T(8,128)(2,1)S(1)}, f32[48,256]{1,0:T(8,128)S(1)}) custom-call(s32[27]{0:T(128)S(1)} %copy-done.5, f32[24,648]{1,0:T(8,128)S(1)} %copy-done.4, f32[648,576]{1,0:T(8,128)S(1)} %bitcast.13, f32[192,128]{1,0:T(8,128)S(1)} %get-tuple-element.10.pos_ref, f32[192,128]{1,0:T(8,128)S(1)} %get-tuple-element.11.mom_ref), custom_call_target="tpu_custom_call" | custom-call | flops 956301312 | bytes 4291436 | tf_op jit(solution)/shard_map/inner/pallas_call | solution.py:287
  12.8 0.0 collective-permute-done.far_ref
  12.8 0.0 collective-permute-done.1.near_ref
  12.8 0.0 copy-start
  12.8 2.6 %outer.1 = f32[576,128]{1,0:T(8,128)S(1)} custom-call(bf16[608,2048]{1,0:T(8,128)(2,1)S(1)} %get-tuple-element.12.w_ref, f32[192,128]{1,0:T(8,128)S(1)} %get-tuple-element.10.pos_ref, f32[192,128]{1,0:T(8,128)S(1)} %get-tuple-element.11.mom_ref, f32[48,256]{1,0:T(8,128)S(1)} %get-tuple-element.13.half_ref, f32[144,128]{1,0:T(8,128)S(1)} %collective-permute-done.far_ref, ...), custom_call_target="tpu_custom_call" | custom-call | flops 1912602624 | bytes 3178496 | tf_op jit(solution)/shard_map/outer/pallas_call | solution.py:287
  15.5 22.0 %all_to_all.10 = f32[16,9,4,128]{3,2,1,0:T(4,128)S(1)} all-to-all(f32[16,9,4,128]{3,2,1,0:T(4,128)S(1)} %bitcast.11), channel_id=1, replica_groups=mesh['bead'=16,'dom'=32] {'bead'}, dimensions={0} | all-to-all | bytes 589824 | tf_op jit(solution)/shard_map/all_to_all | solution.py:339
  37.5 0.0 copy-done
  37.5 0.4 beads.1
  37.9 14.3 %all_to_all.11 = f32[16,15,2,128]{3,2,1,0:T(2,128)S(1)} all-to-all(f32[16,15,2,128]{3,2,1,0:T(2,128)S(1)} %bitcast.10), channel_id=1, replica_groups=mesh['bead'=16,'dom'=32] {'bead'}, dimensions={0} | all-to-all | bytes 491520 | tf_op jit(solution)/shard_map/all_to_all | solution.py:344
  52.2 3.3 %last.1 = (f32[192,128]{1,0:T(8,128)}, f32[192,128]{1,0:T(8,128)}) custom-call(bf16[608,2048]{1,0:T(8,128)(2,1)S(1)} %get-tuple-element.12.w_ref, f32[480,128]{1,0:T(8,128)S(1)} %bitcast.12), custom_call_target="tpu_custom_call" | custom-call | flops 1912602624 | bytes 2932736 | tf_op jit(solution)/shard_map/last/pallas_call | solution.py:287
  (2 shorter events, 0.0 us)
Async XLA Ops:
  0.6 0.9 %copy-start.3 = (f32[2,24,4,128]{3,2,1,0:T(4,128)S(1)}, f32[2,24,4,128]{3,2,1,0:T(4,128)}, u32[]{:S(2)}) copy-start(f32[2,24,4,128]{3,2,1,0:T(4,128)} %param.7) | copy-start | bytes 294916
  0.6 0.9 %copy-start.2 = (f32[2,24,4,128]{3,2,1,0:T(4,128)S(1)}, f32[2,24,4,128]{3,2,1,0:T(4,128)}, u32[]{:S(2)}) copy-start(f32[2,24,4,128]{3,2,1,0:T(4,128)} %param.6) | copy-start | bytes 294916
  1.6 8.5 %copy-start.1 = (f32[576,648]{0,1:T(8,128)S(1)}, f32[576,648]{0,1:T(8,128)}, u32[]{:S(2)}) copy-start(f32[576,648]{0,1:T(8,128)} %param.10) | copy-start | bytes 4478980
  1.6 8.5 %copy-start.4 = (f32[24,648]{1,0:T(8,128)S(1)}, f32[24,648]{1,0:T(8,128)}, u32[]{:S(2)}) copy-start(f32[24,648]{1,0:T(8,128)} %harm_ref.1) | copy-start | bytes 186628
  1.6 8.5 %copy-start.5 = (s32[27]{0:T(128)S(1)}, s32[27]{0:T(128)}, u32[]{:S(2)}) copy-start(s32[27]{0:T(128)} %off_ref.1) | copy-start | bytes 328
  1.6 11.2 %collective-permute-start = (f32[144,128]{1,0:T(8,128)S(1)}, f32[144,128]{1,0:T(8,128)S(1)}, u32[]{:S(2)}, u32[]{:S(2)}) collective-permute-start(f32[144,128]{1,0:T(8,128)S(1)} %get-tuple-element.14), channel_id=1, source_target_pairs={{1,2},{3,4},{5,6},{7,8},{9,10},{11,12},{13,14},{15,16},{17,18},{19... | collective-permute-start | bytes 221192 | tf_op jit(solution)/shard_map/ppermute | solution.py:314
  8.1 4.7 %collective-permute-start.1 = (f32[144,128]{1,0:T(8,128)S(1)}, f32[144,128]{1,0:T(8,128)S(1)}, u32[]{:S(2)}, u32[]{:S(2)}) collective-permute-start(f32[144,128]{1,0:T(8,128)S(1)} %get-tuple-element.15), channel_id=1, source_target_pairs={{0,1},{1,0},{2,3},{3,2},{4,5},{5,4},{6,7},{7,6},{8,9},{9,8},{10,11... | collective-permute-start | bytes 221192 | tf_op jit(solution)/shard_map/ppermute | solution.py:315
  12.8 24.6 %copy-start = (f32[64,64]{1,0:T(8,128)S(1)}, f32[64,64]{1,0:T(8,128)}, u32[]{:S(2)}) copy-start(f32[64,64]{1,0:T(8,128)} %constant.2.clone.map_ref) | copy-start | bytes 49156

commit v5 on v4

--- a/solution.py
+++ b/solution.py
@@ -64,7 +64,7 @@
     return whole[np.ix_(order, order)].astype(np.float32)
 
 
-def put_neighbours(ns_ref, row, bead, field):
+def neighbours(field):
     z = lax.broadcasted_iota(jnp.int32, field.shape, 1) % CZ
     up = jnp.where(z == CZ - 1, pltpu.roll(field, CZ - 1, 1), pltpu.roll(field, CELLS - 1, 1))
     down = jnp.where(z == 0, pltpu.roll(field, CELLS - CZ + 1, 1), pltpu.roll(field, 1, 1))
@@ -75,33 +75,22 @@
     parts.append(jnp.zeros((PART - NEAR, CELLS), f32))
     stack = jnp.concatenate(parts, 0)
     high = stack.astype(bf16)
-    low = (stack - high.astype(f32)).astype(bf16)
-    lanes = pl.ds(bead * CELLS, CELLS)
-    ns_ref[pl.ds(row, PART), lanes] = low
-    ns_ref[pl.ds(row + PART, PART), lanes] = high
-
-
-def put_quad(ns_ref, row, fields):
+    return (stack - high.astype(f32)).astype(bf16), high
+
+
+def two_rows(w_ref, fields):
+    sums = []
     for bead in range(2):
         d0, d1, d2, d3 = (plane[bead] for plane in fields)
-        for q, field in enumerate((d0 - d2, d1 + d2, d2 - d1, d1 - d3)):
-            put_neighbours(ns_ref, row + q * POINT, bead, field)
-
-
-def two_rows(w_ref, ns_ref, row):
+        sums.append((d0 - d2, d1 + d2, d2 - d1, d1 - d3))
     m = []
     for q in range(4):
-        high = jnp.dot(
-            w_ref[:, q * POINT : q * POINT + PART],
-            ns_ref[pl.ds(row + q * POINT + PART, PART), :],
-            preferred_element_type=f32,
+        low, high = (jnp.concatenate(parts, 1) for parts in zip(*(neighbours(sums[bead][q]) for bead in range(2))))
+        whole = jnp.dot(w_ref[:, q * POINT : q * POINT + PART], high, preferred_element_type=f32)
+        rest = jnp.dot(
+            w_ref[:, q * POINT : (q + 1) * POINT], jnp.concatenate([low, high], 0), preferred_element_type=f32
         )
-        rest = jnp.dot(
-            w_ref[:, q * POINT : (q + 1) * POINT],
-            ns_ref[pl.ds(row + q * POINT, POINT), :],
-            preferred_element_type=f32,
-        )
-        m.append(high + rest)
+        m.append(whole + rest)
     return m[0] + (m[1] + m[2]), (m[1] - m[2]) - m[3]
 
 
@@ -154,8 +143,8 @@
             near_ref[rows, :] = halves(core, right, left)
 
 
-def inner_kernel(off_ref, harm_ref, cub_ref, pos_ref, mom_ref, w_ref, half_ref, order, hpad, tail, cat, ns):
-    put_quad(ns, 0, [[block(pos_ref, plane, bead) for bead in range(2)] for plane in range(OWN)])
+def inner_kernel(off_ref, harm_ref, cub_ref, pos_ref, mom_ref, w_ref, half_ref, order, hpad, tail):
+    fields = [[block(pos_ref, plane, bead) for bead in range(2)] for plane in range(OWN)]
     for o in range(NOFF):
         order[o] = 0
     for o in range(NOFF):
@@ -170,6 +159,7 @@
         rows = pl.ds(pl.multiple_of(order[code] * COMP, 8), COMP)
         return jnp.concatenate([cub_ref[rows, 0:512], tail[rows, :]], 1)
 
+    points = [[] for _ in range(8)]
     for s in range(0, 9, 2):
         shifts = range(s, min(s + 2, 9))
         before, here, after = (
@@ -180,15 +170,11 @@
             if len(shifts) == 1:
                 weight = jnp.concatenate([weight, jnp.zeros((PART - NEAR, 640), f32)], 0)
             high = weight.astype(bf16)
-            rows = pl.ds(q * POINT + s * COMP, weight.shape[0])
-            cat[rows, :] = high
-            rows = pl.ds(q * POINT + PART + s * COMP, weight.shape[0])
-            cat[rows, :] = (weight - high.astype(f32)).astype(bf16)
-    for m in range(0, ROWS, 128):
-        size = min(128, ROWS - m)
-        for k in range(0, QUAD, 128):
-            w_ref[m : m + size, k : k + 128] = cat[k : k + 128, m : m + 128].T[:size]
-    for plane, rows in zip((1, 2), two_rows(w_ref, ns, 0)):
+            points[2 * q].append(high)
+            points[2 * q + 1].append((weight - high.astype(f32)).astype(bf16))
+    for i, parts in enumerate(points):
+        w_ref[:, i * PART : (i + 1) * PART] = jnp.concatenate(parts, 0).T[:ROWS]
+    for plane, rows in zip((1, 2), two_rows(w_ref, fields)):
         force = force_from(rows, pair(pos_ref, plane))
         half_ref[(plane - 1) * COMP : plane * COMP, :] = pair(mom_ref, plane) + KICK * force
 
@@ -197,7 +183,7 @@
     return (0, plane) if plane < 3 else (1, EXT - 1 - plane)
 
 
-def outer_kernel(w_ref, pos_ref, mom_ref, half_ref, far_ref, near_ref, send_ref, ns):
+def outer_kernel(w_ref, pos_ref, mom_ref, half_ref, far_ref, near_ref, send_ref):
     core = lax.axis_index("dom") % 2
     left = [[halves(core, block(far_ref, i, bead), block(near_ref, i, bead)) for bead in range(2)] for i in range(3)]
     right = [[halves(core, block(near_ref, i, bead), block(far_ref, i, bead)) for bead in range(2)] for i in range(3)]
@@ -220,16 +206,15 @@
         half, step = place_of(plane + 1)
         send_ref[pl.ds(half * 288 + step * 4 + kind * 2 + bead, COMP, stride=12), :] = value
 
-    for i, first in enumerate((-1, OWN - 1)):
-        put_quad(ns, i * QUAD, [[position(first + n, bead) for bead in range(2)] for n in range(-1, 3)])
     for plane in range(-1, OWN + 1):
         for bead in range(2):
             store(plane, 0, bead, position(plane, bead))
     for plane in (1, 2):
         for bead in range(2):
             store(plane, 1, bead, half_ref[(plane - 1) * COMP : plane * COMP, bead * CELLS : (bead + 1) * CELLS])
-    for i, first in enumerate((-1, OWN - 1)):
-        for plane, rows in zip((first, first + 1), two_rows(w_ref, ns, i * QUAD)):
+    for first in (-1, OWN - 1):
+        fields = [[position(first + n, bead) for bead in range(2)] for n in range(-1, 3)]
+        for plane, rows in zip((first, first + 1), two_rows(w_ref, fields)):
             force = force_from(rows, jnp.concatenate([position(plane, bead) for bead in range(2)], 1))
             for bead in range(2):
                 half = momentum(plane, bead) + KICK * force[:, bead * CELLS : (bead + 1) * CELLS]
@@ -256,7 +241,7 @@
                 ]
 
 
-def last_kernel(w_ref, in_ref, pos_hbm, mom_hbm, pos_ref, mom_ref, ns, sem):
+def last_kernel(w_ref, in_ref, pos_hbm, mom_hbm, pos_ref, mom_ref, sem):
     def value(plane, kind, bead):
         half, step = place_of(plane)
         row = step * 2 + bead if kind == 0 else 6 + (step - 1) * 2 + bead
@@ -267,10 +252,9 @@
             pos_ref[pl.ds(bead * COMP * OWN + plane - 1, COMP, stride=OWN), :] = value(plane, 0, bead)
     out = pltpu.make_async_copy(pos_ref, pos_hbm, sem.at[0])
     out.start()
-    for i, first in enumerate((1, 3)):
-        put_quad(ns, i * QUAD, [[value(first + n, 0, bead) for bead in range(2)] for n in range(-1, 3)])
-    for i, first in enumerate((1, 3)):
-        for plane, rows in zip((first, first + 1), two_rows(w_ref, ns, i * QUAD)):
+    for first in (1, 3):
+        fields = [[value(first + n, 0, bead) for bead in range(2)] for n in range(-1, 3)]
+        for plane, rows in zip((first, first + 1), two_rows(w_ref, fields)):
             force = force_from(rows, jnp.concatenate([value(plane, 0, bead) for bead in range(2)], 1))
             for bead in range(2):
                 mom_ref[pl.ds(bead * COMP * OWN + plane - 1, COMP, stride=OWN), :] = (
@@ -294,10 +278,6 @@
         compiler_params=pltpu.CompilerParams(vmem_limit_bytes=24 * 1024 * 1024),
         cost_estimate=pl.CostEstimate(flops=flops, bytes_accessed=size, transcendentals=0),
     )(*args)
-
-
-def neighbours(quads):
-    return pltpu.VMEM((quads * QUAD, 2 * CELLS), bf16)
 
 
 def body(positions, momenta, offsets, harmonic, cubic):
@@ -322,8 +302,6 @@
             pltpu.SMEM((NOFF,), jnp.int32),
             pltpu.VMEM((128, 768), f32),
             pltpu.VMEM((768, 128), f32),
-            pltpu.VMEM((QUAD, 640), bf16),
-            neighbours(1),
         ],
         2 * per_plane,
         offsets,
@@ -333,7 +311,7 @@
         mom,
     )
     (send,) = call(
-        outer_kernel, "outer", [VMEM] * 6, [shape((GROUP * 36, CELLS), f32)], [neighbours(2)], 4 * per_plane,
+        outer_kernel, "outer", [VMEM] * 6, [shape((GROUP * 36, CELLS), f32)], [], 4 * per_plane,
         weights, pos, mom, half, far, near,
     )
     got = lax.all_to_all(send.reshape(GROUP, 9, 4, CELLS), "bead", 0, 0, tiled=True)
@@ -344,7 +322,7 @@
     got = lax.all_to_all(back.reshape(GROUP, 15, 2, CELLS), "bead", 0, 0, tiled=True)
     new_pos, new_mom = call(
         last_kernel, "last", [VMEM] * 2, [own] * 2,
-        [pltpu.VMEM(own.shape, f32), pltpu.VMEM(own.shape, f32), neighbours(2), pltpu.SemaphoreType.DMA((2,))],
+        [pltpu.VMEM(own.shape, f32), pltpu.VMEM(own.shape, f32), pltpu.SemaphoreType.DMA((2,))],
         4 * per_plane, weights, got.reshape(GROUP * 30, CELLS), to=HBM,
     )
     return new_pos.reshape(positions.shape), new_mom.reshape(momenta.shape)

time: 55.7 us -> 55.2 us (level)
  transfers between devices with their start and end apart: 2 -> 2, of which waited for: 0 -> 0; matrix products, arithmetic and copies ran while one was open for 0% -> 0% of each run, Pallas kernels for 5% -> 4%
where the time goes in v5:
time: 55.2 us; the launch traced here: 54.9 us
  blocking collectives  36.3 us (66%)
  Pallas kernels  8.49 us (15%)
  starting transfers between devices  8.43 us (15%)
  local copies, waits for them, and re-layouts  0.93 us (2%)
  between operations  0.74 us (1%)
    all_to_all x1, blocking collectives, body(): lax.all_to_all(send.reshape(GROUP, 9, 4, CELLS), 'bead', 0, 0, tiled=True)  22 us
    all_to_all x1, blocking collectives, body(): lax.all_to_all(back.reshape(GROUP, 15, 2, CELLS), 'bead', 0, 0, tiled=True)  14.3 us
    pallas_call x6, Pallas kernels, call(): pl.pallas_call(kernel, name=name, in_specs=ins, out_specs=[to] * len(outs...  8.49 us
    ppermute x1, starting transfers between devices, body(): far = lax.ppermute(far, 'dom', between + [(j, i) for i, j in between])  6.51 us
    ppermute x1, starting transfers between devices, body(): near = lax.ppermute(near, 'dom', [(i, i ^ 1) for i in range(doms)])  1.92 us
  transfers between devices with their start and end apart: 2, of which 0 were waited for; matrix products, arithmetic and copies ran while one was open for 0% of the time, Pallas kernels for 4%

profile of v5, /device:TPU:2, one launch (start us, length us, event | category | flops | bytes accessed | tf_op | source)
XLA Modules:
  0.0 54.9 jit_solution(2055616778019727018)
XLA Ops:
  0.6 0.0 copy-start.3
  0.6 0.0 copy-start.2
  0.7 0.9 %copy-done.3 = f32[2,24,4,128]{3,2,1,0:T(4,128)S(1)} copy-done((f32[2,24,4,128]{3,2,1,0:T(4,128)S(1)}, f32[2,24,4,128]{3,2,1,0:T(4,128)}, u32[]{:S(2)}) %copy-start.3) | copy-done | bytes 98328
  1.5 0.0 copy-done.2
  1.6 0.0 copy-start.1
  1.6 0.0 copy-start.4
  1.6 0.0 copy-start.5
  1.6 6.5 %collective-permute-start = (f32[144,128]{1,0:T(8,128)S(1)}, f32[144,128]{1,0:T(8,128)S(1)}, u32[]{:S(2)}, u32[]{:S(2)}) collective-permute-start(f32[144,128]{1,0:T(8,128)S(1)} %get-tuple-element.14), channel_id=1, source_target_pairs={{1,2},{3,4},{5,6},{7,8},{9,10},{11,12},{13,14},{15,16},{17,18},{19... | collective-permute-start | bytes 221192 | tf_op jit(solution)/shard_map/ppermute | solution.py:294
  8.1 1.9 %collective-permute-start.1 = (f32[144,128]{1,0:T(8,128)S(1)}, f32[144,128]{1,0:T(8,128)S(1)}, u32[]{:S(2)}, u32[]{:S(2)}) collective-permute-start(f32[144,128]{1,0:T(8,128)S(1)} %get-tuple-element.15), channel_id=1, source_target_pairs={{0,1},{1,0},{2,3},{3,2},{4,5},{5,4},{6,7},{7,6},{8,9},{9,8},{10,11... | collective-permute-start | bytes 221192 | tf_op jit(solution)/shard_map/ppermute | solution.py:295
  10.1 0.0 copy-done.1
  10.1 0.0 copy-done.4
  10.1 0.0 copy-done.5
  10.1 2.3 %inner.1 = (bf16[608,2048]{1,0:T(8,128)(2,1)S(1)}, f32[48,256]{1,0:T(8,128)S(1)}) custom-call(s32[27]{0:T(128)S(1)} %copy-done.5, f32[24,648]{1,0:T(8,128)S(1)} %copy-done.4, f32[648,576]{1,0:T(8,128)S(1)} %bitcast.13, f32[192,128]{1,0:T(8,128)S(1)} %get-tuple-element.10.pos_ref, f32[192,128]{1,0:T(8,128)S(1)} %get-tuple-element.11.mom_ref), custom_call_target="tpu_custom_call" | custom-call | flops 956301312 | bytes 4291436 | tf_op jit(solution)/shard_map/inner/pallas_call | solution.py:271
  12.4 0.0 collective-permute-done.far_ref
  12.4 0.0 collective-permute-done.1.near_ref
  12.4 0.0 copy-start
  12.4 2.6 %outer.1 = f32[576,128]{1,0:T(8,128)S(1)} custom-call(bf16[608,2048]{1,0:T(8,128)(2,1)S(1)} %get-tuple-element.12.w_ref, f32[192,128]{1,0:T(8,128)S(1)} %get-tuple-element.10.pos_ref, f32[192,128]{1,0:T(8,128)S(1)} %get-tuple-element.11.mom_ref, f32[48,256]{1,0:T(8,128)S(1)} %get-tuple-element.13.half_ref, f32[144,128]{1,0:T(8,128)S(1)} %collective-permute-done.far_ref, ...), custom_call_target="tpu_custom_call" | custom-call | flops 1912602624 | bytes 3178496 | tf_op jit(solution)/shard_map/outer/pallas_call | solution.py:271
  15.0 22.0 %all_to_all.10 = f32[16,9,4,128]{3,2,1,0:T(4,128)S(1)} all-to-all(f32[16,9,4,128]{3,2,1,0:T(4,128)S(1)} %bitcast.11), channel_id=1, replica_groups=mesh['bead'=16,'dom'=32] {'bead'}, dimensions={0} | all-to-all | bytes 589824 | tf_op jit(solution)/shard_map/all_to_all | solution.py:317
  37.0 0.0 copy-done
  37.0 0.4 beads.1
  37.4 14.3 %all_to_all.11 = f32[16,15,2,128]{3,2,1,0:T(2,128)S(1)} all-to-all(f32[16,15,2,128]{3,2,1,0:T(2,128)S(1)} %bitcast.10), channel_id=1, replica_groups=mesh['bead'=16,'dom'=32] {'bead'}, dimensions={0} | all-to-all | bytes 491520 | tf_op jit(solution)/shard_map/all_to_all | solution.py:322
  51.7 3.2 %last.1 = (f32[192,128]{1,0:T(8,128)}, f32[192,128]{1,0:T(8,128)}) custom-call(bf16[608,2048]{1,0:T(8,128)(2,1)S(1)} %get-tuple-element.12.w_ref, f32[480,128]{1,0:T(8,128)S(1)} %bitcast.12), custom_call_target="tpu_custom_call" | custom-call | flops 1912602624 | bytes 2932736 | tf_op jit(solution)/shard_map/last/pallas_call | solution.py:271
  (2 shorter events, 0.0 us)
Async XLA Ops:
  0.6 0.9 %copy-start.3 = (f32[2,24,4,128]{3,2,1,0:T(4,128)S(1)}, f32[2,24,4,128]{3,2,1,0:T(4,128)}, u32[]{:S(2)}) copy-start(f32[2,24,4,128]{3,2,1,0:T(4,128)} %param.7) | copy-start | bytes 294916
  0.6 0.9 %copy-start.2 = (f32[2,24,4,128]{3,2,1,0:T(4,128)S(1)}, f32[2,24,4,128]{3,2,1,0:T(4,128)}, u32[]{:S(2)}) copy-start(f32[2,24,4,128]{3,2,1,0:T(4,128)} %param.6) | copy-start | bytes 294916
  1.6 8.5 %copy-start.1 = (f32[576,648]{0,1:T(8,128)S(1)}, f32[576,648]{0,1:T(8,128)}, u32[]{:S(2)}) copy-start(f32[576,648]{0,1:T(8,128)} %param.10) | copy-start | bytes 4478980
  1.6 8.5 %copy-start.4 = (f32[24,648]{1,0:T(8,128)S(1)}, f32[24,648]{1,0:T(8,128)}, u32[]{:S(2)}) copy-start(f32[24,648]{1,0:T(8,128)} %harm_ref.1) | copy-start | bytes 186628
  1.6 8.5 %copy-start.5 = (s32[27]{0:T(128)S(1)}, s32[27]{0:T(128)}, u32[]{:S(2)}) copy-start(s32[27]{0:T(128)} %off_ref.1) | copy-start | bytes 328
  1.6 10.8 %collective-permute-start = (f32[144,128]{1,0:T(8,128)S(1)}, f32[144,128]{1,0:T(8,128)S(1)}, u32[]{:S(2)}, u32[]{:S(2)}) collective-permute-start(f32[144,128]{1,0:T(8,128)S(1)} %get-tuple-element.14), channel_id=1, source_target_pairs={{1,2},{3,4},{5,6},{7,8},{9,10},{11,12},{13,14},{15,16},{17,18},{19... | collective-permute-start | bytes 221192 | tf_op jit(solution)/shard_map/ppermute | solution.py:294
  8.1 4.3 %collective-permute-start.1 = (f32[144,128]{1,0:T(8,128)S(1)}, f32[144,128]{1,0:T(8,128)S(1)}, u32[]{:S(2)}, u32[]{:S(2)}) collective-permute-start(f32[144,128]{1,0:T(8,128)S(1)} %get-tuple-element.15), channel_id=1, source_target_pairs={{0,1},{1,0},{2,3},{3,2},{4,5},{5,4},{6,7},{7,6},{8,9},{9,8},{10,11... | collective-permute-start | bytes 221192 | tf_op jit(solution)/shard_map/ppermute | solution.py:295
  12.4 24.6 %copy-start = (f32[64,64]{1,0:T(8,128)S(1)}, f32[64,64]{1,0:T(8,128)}, u32[]{:S(2)}) copy-start(f32[64,64]{1,0:T(8,128)} %constant.2.clone.map_ref) | copy-start | bytes 49156

commit v6 on v5

--- a/solution.py
+++ b/solution.py
@@ -62,6 +62,13 @@
     per = count // groups
     order = np.arange(2 * count).reshape(2, groups, per).transpose(0, 2, 1).reshape(-1)
     return whole[np.ix_(order, order)].astype(np.float32)
+
+
+def bead_map():
+    whole = propagator(GROUP)
+    high = whole.astype(bf16)
+    low = (whole - high.astype(np.float32)).astype(bf16)
+    return jnp.asarray(np.concatenate([high, high, low], 1))
 
 
 def neighbours(field):
@@ -225,12 +232,10 @@
     columns = []
     for r in range(9):
         columns.append(jnp.concatenate([in_ref[pl.ds(r * 4 + q, GROUP, stride=36), :] for q in range(4)], 0))
-    moved = jnp.dot(
-        map_ref[...],
-        jnp.concatenate(columns, 1),
-        precision=lax.Precision.HIGHEST,
-        preferred_element_type=f32,
-    )
+    rows = jnp.concatenate(columns, 1)
+    high = rows.astype(bf16)
+    low = (rows - high.astype(f32)).astype(bf16)
+    moved = jnp.dot(map_ref[...], jnp.concatenate([high, low, high], 0), preferred_element_type=f32)
     for r in range(9):
         line, step = r // 3, r % 3
         for q in range(4):
@@ -317,7 +322,7 @@
     got = lax.all_to_all(send.reshape(GROUP, 9, 4, CELLS), "bead", 0, 0, tiled=True)
     (back,) = call(
         bead_kernel, "beads", [VMEM] * 2, [shape((GROUP * 30, CELLS), f32)], [], 2 * 64 * 64 * 9 * CELLS,
-        jnp.asarray(propagator(GROUP)), got.reshape(GROUP * 36, CELLS),
+        bead_map(), got.reshape(GROUP * 36, CELLS),
     )
     got = lax.all_to_all(back.reshape(GROUP, 15, 2, CELLS), "bead", 0, 0, tiled=True)
     new_pos, new_mom = call(

time: 55.2 us -> 55 us (level)
  no operation moved by 1% of the time
where the time goes in v6:
time: 55 us; the launch traced here: 54.8 us
  blocking collectives  36.3 us (66%)
  starting transfers between devices  8.43 us (15%)
  Pallas kernels  8.32 us (15%)
  local copies, waits for them, and re-layouts  0.93 us (2%)
  between operations  0.74 us (1%)
    all_to_all x1, blocking collectives, body(): lax.all_to_all(send.reshape(GROUP, 9, 4, CELLS), 'bead', 0, 0, tiled=True)  22 us
    all_to_all x1, blocking collectives, body(): lax.all_to_all(back.reshape(GROUP, 15, 2, CELLS), 'bead', 0, 0, tiled=True)  14.3 us
    pallas_call x6, Pallas kernels, call(): pl.pallas_call(kernel, name=name, in_specs=ins, out_specs=[to] * len(outs...  8.32 us
    ppermute x1, starting transfers between devices, body(): far = lax.ppermute(far, 'dom', between + [(j, i) for i, j in between])  6.51 us
    ppermute x1, starting transfers between devices, body(): near = lax.ppermute(near, 'dom', [(i, i ^ 1) for i in range(doms)])  1.92 us
  transfers between devices with their start and end apart: 2, of which 0 were waited for; matrix products, arithmetic and copies ran while one was open for 0% of the time, Pallas kernels for 4%

profile of v6, /device:TPU:2, one launch (start us, length us, event | category | flops | bytes accessed | tf_op | source)
XLA Modules:
  0.0 54.8 jit_solution(8675476173415831544)
XLA Ops:
  0.6 0.0 copy-start.3
  0.6 0.0 copy-start.2
  0.7 0.9 %copy-done.3 = f32[2,24,4,128]{3,2,1,0:T(4,128)S(1)} copy-done((f32[2,24,4,128]{3,2,1,0:T(4,128)S(1)}, f32[2,24,4,128]{3,2,1,0:T(4,128)}, u32[]{:S(2)}) %copy-start.3) | copy-done | bytes 98328
  1.5 0.0 copy-done.2
  1.6 0.0 copy-start.1
  1.6 0.0 copy-start.4
  1.6 0.0 copy-start.5
  1.6 6.5 %collective-permute-start = (f32[144,128]{1,0:T(8,128)S(1)}, f32[144,128]{1,0:T(8,128)S(1)}, u32[]{:S(2)}, u32[]{:S(2)}) collective-permute-start(f32[144,128]{1,0:T(8,128)S(1)} %get-tuple-element.14), channel_id=1, source_target_pairs={{1,2},{3,4},{5,6},{7,8},{9,10},{11,12},{13,14},{15,16},{17,18},{19... | collective-permute-start | bytes 221192 | tf_op jit(solution)/shard_map/ppermute | solution.py:299
  8.1 1.9 %collective-permute-start.1 = (f32[144,128]{1,0:T(8,128)S(1)}, f32[144,128]{1,0:T(8,128)S(1)}, u32[]{:S(2)}, u32[]{:S(2)}) collective-permute-start(f32[144,128]{1,0:T(8,128)S(1)} %get-tuple-element.15), channel_id=1, source_target_pairs={{0,1},{1,0},{2,3},{3,2},{4,5},{5,4},{6,7},{7,6},{8,9},{9,8},{10,11... | collective-permute-start | bytes 221192 | tf_op jit(solution)/shard_map/ppermute | solution.py:300
  10.1 0.0 copy-done.1
  10.1 0.0 copy-done.4
  10.1 0.0 copy-done.5
  10.1 2.3 %inner.1 = (bf16[608,2048]{1,0:T(8,128)(2,1)S(1)}, f32[48,256]{1,0:T(8,128)S(1)}) custom-call(s32[27]{0:T(128)S(1)} %copy-done.5, f32[24,648]{1,0:T(8,128)S(1)} %copy-done.4, f32[648,576]{1,0:T(8,128)S(1)} %bitcast.13, f32[192,128]{1,0:T(8,128)S(1)} %get-tuple-element.10.pos_ref, f32[192,128]{1,0:T(8,128)S(1)} %get-tuple-element.11.mom_ref), custom_call_target="tpu_custom_call" | custom-call | flops 956301312 | bytes 4291436 | tf_op jit(solution)/shard_map/inner/pallas_call | solution.py:276
  12.4 0.0 collective-permute-done.far_ref
  12.4 0.0 collective-permute-done.1.near_ref
  12.4 0.0 copy-start
  12.4 2.6 %outer.1 = f32[576,128]{1,0:T(8,128)S(1)} custom-call(bf16[608,2048]{1,0:T(8,128)(2,1)S(1)} %get-tuple-element.12.w_ref, f32[192,128]{1,0:T(8,128)S(1)} %get-tuple-element.10.pos_ref, f32[192,128]{1,0:T(8,128)S(1)} %get-tuple-element.11.mom_ref, f32[48,256]{1,0:T(8,128)S(1)} %get-tuple-element.13.half_ref, f32[144,128]{1,0:T(8,128)S(1)} %collective-permute-done.far_ref, ...), custom_call_target="tpu_custom_call" | custom-call | flops 1912602624 | bytes 3178496 | tf_op jit(solution)/shard_map/outer/pallas_call | solution.py:276
  15.0 22.0 %all_to_all.10 = f32[16,9,4,128]{3,2,1,0:T(4,128)S(1)} all-to-all(f32[16,9,4,128]{3,2,1,0:T(4,128)S(1)} %bitcast.11), channel_id=1, replica_groups=mesh['bead'=16,'dom'=32] {'bead'}, dimensions={0} | all-to-all | bytes 589824 | tf_op jit(solution)/shard_map/all_to_all | solution.py:322
  37.0 0.0 copy-done
  37.0 0.2 beads.1
  37.2 14.3 %all_to_all.11 = f32[16,15,2,128]{3,2,1,0:T(2,128)S(1)} all-to-all(f32[16,15,2,128]{3,2,1,0:T(2,128)S(1)} %bitcast.10), channel_id=1, replica_groups=mesh['bead'=16,'dom'=32] {'bead'}, dimensions={0} | all-to-all | bytes 491520 | tf_op jit(solution)/shard_map/all_to_all | solution.py:327
  51.5 3.2 %last.1 = (f32[192,128]{1,0:T(8,128)}, f32[192,128]{1,0:T(8,128)}) custom-call(bf16[608,2048]{1,0:T(8,128)(2,1)S(1)} %get-tuple-element.12.w_ref, f32[480,128]{1,0:T(8,128)S(1)} %bitcast.12), custom_call_target="tpu_custom_call" | custom-call | flops 1912602624 | bytes 2932736 | tf_op jit(solution)/shard_map/last/pallas_call | solution.py:276
  (2 shorter events, 0.0 us)
Async XLA Ops:
  0.6 0.9 %copy-start.3 = (f32[2,24,4,128]{3,2,1,0:T(4,128)S(1)}, f32[2,24,4,128]{3,2,1,0:T(4,128)}, u32[]{:S(2)}) copy-start(f32[2,24,4,128]{3,2,1,0:T(4,128)} %param.7) | copy-start | bytes 294916
  0.6 0.9 %copy-start.2 = (f32[2,24,4,128]{3,2,1,0:T(4,128)S(1)}, f32[2,24,4,128]{3,2,1,0:T(4,128)}, u32[]{:S(2)}) copy-start(f32[2,24,4,128]{3,2,1,0:T(4,128)} %param.6) | copy-start | bytes 294916
  1.6 8.5 %copy-start.1 = (f32[576,648]{0,1:T(8,128)S(1)}, f32[576,648]{0,1:T(8,128)}, u32[]{:S(2)}) copy-start(f32[576,648]{0,1:T(8,128)} %param.10) | copy-start | bytes 4478980
  1.6 8.5 %copy-start.4 = (f32[24,648]{1,0:T(8,128)S(1)}, f32[24,648]{1,0:T(8,128)}, u32[]{:S(2)}) copy-start(f32[24,648]{1,0:T(8,128)} %harm_ref.1) | copy-start | bytes 186628
  1.6 8.5 %copy-start.5 = (s32[27]{0:T(128)S(1)}, s32[27]{0:T(128)}, u32[]{:S(2)}) copy-start(s32[27]{0:T(128)} %off_ref.1) | copy-start | bytes 328
  1.6 10.8 %collective-permute-start = (f32[144,128]{1,0:T(8,128)S(1)}, f32[144,128]{1,0:T(8,128)S(1)}, u32[]{:S(2)}, u32[]{:S(2)}) collective-permute-start(f32[144,128]{1,0:T(8,128)S(1)} %get-tuple-element.14), channel_id=1, source_target_pairs={{1,2},{3,4},{5,6},{7,8},{9,10},{11,12},{13,14},{15,16},{17,18},{19... | collective-permute-start | bytes 221192 | tf_op jit(solution)/shard_map/ppermute | solution.py:299
  8.1 4.3 %collective-permute-start.1 = (f32[144,128]{1,0:T(8,128)S(1)}, f32[144,128]{1,0:T(8,128)S(1)}, u32[]{:S(2)}, u32[]{:S(2)}) collective-permute-start(f32[144,128]{1,0:T(8,128)S(1)} %get-tuple-element.15), channel_id=1, source_target_pairs={{0,1},{1,0},{2,3},{3,2},{4,5},{5,4},{6,7},{7,6},{8,9},{9,8},{10,11... | collective-permute-start | bytes 221192 | tf_op jit(solution)/shard_map/ppermute | solution.py:300
  12.4 24.6 %copy-start = (bf16[64,192]{1,0:T(8,128)(2,1)S(1)}, bf16[64,192]{1,0:T(8,128)(2,1)}, u32[]{:S(2)}) copy-start(bf16[64,192]{1,0:T(8,128)(2,1)} %constant.2.clone.map_ref) | copy-start | bytes 73732

commit v7 on v6

--- a/solution.py
+++ b/solution.py
@@ -193,7 +193,7 @@
 def outer_kernel(w_ref, pos_ref, mom_ref, half_ref, far_ref, near_ref, send_ref):
     core = lax.axis_index("dom") % 2
     left = [[halves(core, block(far_ref, i, bead), block(near_ref, i, bead)) for bead in range(2)] for i in range(3)]
-    right = [[halves(core, block(near_ref, i, bead), block(far_ref, i, bead)) for bead in range(2)] for i in range(3)]
+    right = [[halves(core, block(near_ref, i + 3, bead), block(far_ref, i, bead)) for bead in range(2)] for i in range(3)]
 
     def position(plane, bead):
         if plane < 0:
@@ -297,7 +297,7 @@
     far, near, pos, mom = call(pack_kernel, "pack", [VMEM] * 3, [halo, halo, own, own], [], EARLY, blank, pos, mom)
     between = [(i, (i + 1) % doms) for i in range(1, doms, 2)]
     far = lax.ppermute(far, "dom", between + [(j, i) for i, j in between])
-    near = lax.ppermute(near, "dom", [(i, i ^ 1) for i in range(doms)])
+    near = lax.all_gather(near, "dom", axis_index_groups=[[i, i + 1] for i in range(0, doms, 2)], tiled=True)
     weights, half = call(
         inner_kernel,
         "inner",

time: 55 us -> 54.6 us (level)
  the two profiles are of different devices: /device:TPU:2 before, /device:TPU:64 now
where the time goes in v7:
time: 54.6 us; the launch traced here: 54.3 us
  blocking collectives  36.9 us (68%)
  Pallas kernels  8.33 us (15%)
  starting transfers between devices  7.41 us (14%)
  local copies, waits for them, and re-layouts  0.93 us (2%)
  between operations  0.7 us (1%)
    all_to_all x1, blocking collectives, body(): lax.all_to_all(send.reshape(GROUP, 9, 4, CELLS), 'bead', 0, 0, tiled=True)  20.9 us
    all_to_all x1, blocking collectives, body(): lax.all_to_all(back.reshape(GROUP, 15, 2, CELLS), 'bead', 0, 0, tiled=True)  14.1 us
    pallas_call x6, Pallas kernels, call(): pl.pallas_call(kernel, name=name, in_specs=ins, out_specs=[to] * len(outs...  8.33 us
    ppermute x1, starting transfers between devices, body(): far = lax.ppermute(far, 'dom', between + [(j, i) for i, j in between])  7.41 us
    all_gather x1, blocking collectives, body(): lax.all_gather(near, 'dom', axis_index_groups=[[i, i + 1] for i in range(...  1.91 us
  transfers between devices with their start and end apart: 1, of which 0 were waited for; matrix products, arithmetic and copies ran while one was open for 0% of the time, Pallas kernels for 4%

profile of v7, /device:TPU:64, one launch (start us, length us, event | category | flops | bytes accessed | tf_op | source)
XLA Modules:
  0.0 54.3 jit_solution(13006878873913078920)
XLA Ops:
  0.6 0.0 copy-start.3
  0.6 0.0 copy-start.2
  0.7 0.9 %copy-done.3 = f32[2,24,4,128]{3,2,1,0:T(4,128)S(1)} copy-done((f32[2,24,4,128]{3,2,1,0:T(4,128)S(1)}, f32[2,24,4,128]{3,2,1,0:T(4,128)}, u32[]{:S(2)}) %copy-start.3) | copy-done | bytes 98328
  1.5 0.0 copy-done.2
  1.6 0.0 copy-start.1
  1.6 0.0 copy-start.4
  1.6 0.0 copy-start.5
  1.6 7.4 %collective-permute-start = (f32[144,128]{1,0:T(8,128)S(1)}, f32[144,128]{1,0:T(8,128)S(1)}, u32[]{:S(2)}, u32[]{:S(2)}) collective-permute-start(f32[144,128]{1,0:T(8,128)S(1)} %get-tuple-element.14), channel_id=1, source_target_pairs={{1,2},{3,4},{5,6},{7,8},{9,10},{11,12},{13,14},{15,16},{17,18},{19... | collective-permute-start | bytes 221192 | tf_op jit(solution)/shard_map/ppermute | solution.py:299
  9.0 1.9 %all_gather.3.near_ref = f32[288,128]{1,0:T(8,128)S(1)} all-gather(f32[144,128]{1,0:T(8,128)S(1)} %get-tuple-element.15), channel_id=1, replica_groups={{0,1},{2,3},{4,5},{6,7},{8,9},{10,11},{12,13},{14,15},{16,17},{18,19},{..., dimensions={0}, use_global_device_ids=true | all-gather | bytes 221184 | tf_op jit(solution)/shard_map/all_gather | solution.py:300
  10.9 0.0 copy-done.1
  10.9 0.0 copy-done.4
  10.9 0.0 copy-done.5
  11.0 2.3 %inner.1 = (bf16[608,2048]{1,0:T(8,128)(2,1)S(1)}, f32[48,256]{1,0:T(8,128)S(1)}) custom-call(s32[27]{0:T(128)S(1)} %copy-done.5, f32[24,648]{1,0:T(8,128)S(1)} %copy-done.4, f32[648,576]{1,0:T(8,128)S(1)} %bitcast.13, f32[192,128]{1,0:T(8,128)S(1)} %get-tuple-element.10.pos_ref, f32[192,128]{1,0:T(8,128)S(1)} %get-tuple-element.11.mom_ref), custom_call_target="tpu_custom_call" | custom-call | flops 956301312 | bytes 4291436 | tf_op jit(solution)/shard_map/inner/pallas_call | solution.py:276
  13.3 0.0 collective-permute-done.far_ref
  13.3 0.0 copy-start
  13.3 2.6 %outer.1 = f32[576,128]{1,0:T(8,128)S(1)} custom-call(bf16[608,2048]{1,0:T(8,128)(2,1)S(1)} %get-tuple-element.12.w_ref, f32[192,128]{1,0:T(8,128)S(1)} %get-tuple-element.10.pos_ref, f32[192,128]{1,0:T(8,128)S(1)} %get-tuple-element.11.mom_ref, f32[48,256]{1,0:T(8,128)S(1)} %get-tuple-element.13.half_ref, f32[144,128]{1,0:T(8,128)S(1)} %collective-permute-done.far_ref, ...), custom_call_target="tpu_custom_call" | custom-call | flops 1912602624 | bytes 3252224 | tf_op jit(solution)/shard_map/outer/pallas_call | solution.py:276
  15.9 20.9 %all_to_all.10 = f32[16,9,4,128]{3,2,1,0:T(4,128)S(1)} all-to-all(f32[16,9,4,128]{3,2,1,0:T(4,128)S(1)} %bitcast.11), channel_id=1, replica_groups=mesh['bead'=16,'dom'=32] {'bead'}, dimensions={0} | all-to-all | bytes 589824 | tf_op jit(solution)/shard_map/all_to_all | solution.py:322
  36.7 0.0 copy-done
  36.7 0.2 beads.1
  37.0 14.1 %all_to_all.11 = f32[16,15,2,128]{3,2,1,0:T(2,128)S(1)} all-to-all(f32[16,15,2,128]{3,2,1,0:T(2,128)S(1)} %bitcast.10), channel_id=1, replica_groups=mesh['bead'=16,'dom'=32] {'bead'}, dimensions={0} | all-to-all | bytes 491520 | tf_op jit(solution)/shard_map/all_to_all | solution.py:327
  51.1 3.2 %last.1 = (f32[192,128]{1,0:T(8,128)}, f32[192,128]{1,0:T(8,128)}) custom-call(bf16[608,2048]{1,0:T(8,128)(2,1)S(1)} %get-tuple-element.12.w_ref, f32[480,128]{1,0:T(8,128)S(1)} %bitcast.12), custom_call_target="tpu_custom_call" | custom-call | flops 1912602624 | bytes 2932736 | tf_op jit(solution)/shard_map/last/pallas_call | solution.py:276
  (2 shorter events, 0.0 us)
Async XLA Ops:
  0.6 0.9 %copy-start.3 = (f32[2,24,4,128]{3,2,1,0:T(4,128)S(1)}, f32[2,24,4,128]{3,2,1,0:T(4,128)}, u32[]{:S(2)}) copy-start(f32[2,24,4,128]{3,2,1,0:T(4,128)} %param.7) | copy-start | bytes 294916
  0.6 0.9 %copy-start.2 = (f32[2,24,4,128]{3,2,1,0:T(4,128)S(1)}, f32[2,24,4,128]{3,2,1,0:T(4,128)}, u32[]{:S(2)}) copy-start(f32[2,24,4,128]{3,2,1,0:T(4,128)} %param.6) | copy-start | bytes 294916
  1.6 9.4 %copy-start.1 = (f32[576,648]{0,1:T(8,128)S(1)}, f32[576,648]{0,1:T(8,128)}, u32[]{:S(2)}) copy-start(f32[576,648]{0,1:T(8,128)} %param.10) | copy-start | bytes 4478980
  1.6 9.4 %copy-start.4 = (f32[24,648]{1,0:T(8,128)S(1)}, f32[24,648]{1,0:T(8,128)}, u32[]{:S(2)}) copy-start(f32[24,648]{1,0:T(8,128)} %harm_ref.1) | copy-start | bytes 186628
  1.6 9.4 %copy-start.5 = (s32[27]{0:T(128)S(1)}, s32[27]{0:T(128)}, u32[]{:S(2)}) copy-start(s32[27]{0:T(128)} %off_ref.1) | copy-start | bytes 328
  1.6 11.7 %collective-permute-start = (f32[144,128]{1,0:T(8,128)S(1)}, f32[144,128]{1,0:T(8,128)S(1)}, u32[]{:S(2)}, u32[]{:S(2)}) collective-permute-start(f32[144,128]{1,0:T(8,128)S(1)} %get-tuple-element.14), channel_id=1, source_target_pairs={{1,2},{3,4},{5,6},{7,8},{9,10},{11,12},{13,14},{15,16},{17,18},{19... | collective-permute-start | bytes 221192 | tf_op jit(solution)/shard_map/ppermute | solution.py:299
  13.3 23.5 %copy-start = (bf16[64,192]{1,0:T(8,128)(2,1)S(1)}, bf16[64,192]{1,0:T(8,128)(2,1)}, u32[]{:S(2)}) copy-start(bf16[64,192]{1,0:T(8,128)(2,1)} %constant.2.clone.map_ref) | copy-start | bytes 73732
